TPU v7x, 32 devices: a whole 2x2x4 slice. The times are simulated.
32 devices in a mesh: spec: 4 (over y, x), tile: 8 (over z, core).
Axes of the slice: x: 2, y: 2, z: 4, core: 2. Of those that a mesh axis runs over, the one named last changes fastest.
Arguments:
- action: bfloat16 [128, 3072, 256], P('tile', 'spec'), may hold values from 0.099609375 to 2
- east_current: float32 [128, 256], P('tile'), may hold values from -0.4 to 0.4
- north_current: float32 [128, 256], P('tile'), may hold values from -0.4 to 0.4
- sea_mask: int32 [128, 256], P('tile'), may hold values from 0 to 1, as said below
- pattern: int32 [48, 24], replicated, may hold values from 0 to 47, as said below
- table: bfloat16 [48, 64, 64], replicated, may hold values from -0.15625 to 0.15625
Outputs:
- updated: bfloat16 [128, 3072, 256], P('tile', 'spec')
Inputs may be any that keep to these rules, and one draw needn't show every extreme that they name: `sea_mask`: each tile of 16 latitude rows (all 256 longitudes) holds at most 2048 sea points, and in every draw some tile holds exactly 2048. `pattern`: each row names 24 different direction blocks.
All inputs are finite; a program needn't handle non-finite values.
Results may differ from a plain program's by a relative error of at most 0.0043.
Values may be sent and summed in bfloat16 or wider, within the bound.
No kernel may reach another device: no remote copies, remote signals or barrier semaphores. Data moves between devices by JAX's collectives and lax.ppermute only.
A program may use at most 128 MiB of HBM per device.

v0:
```python
import jax
import jax.numpy as jnp
from jax import lax
from jax.sharding import PartitionSpec as P

NF = 64
ND = 48
SUB = 2


courant_scale = 0.45


def extended(cells, sides, width):
    for axis, dim in sides:
        count = lax.axis_size(axis)
        ends = count - 1
        head = lax.slice_in_dim(cells, 0, width, axis=dim)
        tail = lax.slice_in_dim(cells, cells.shape[dim] - width, cells.shape[dim], axis=dim)
        cells = jnp.concatenate(
            [
                lax.ppermute(tail, axis, [(i, (i + 1) % count) for i in range(ends)]),
                cells,
                lax.ppermute(head, axis, [((i + 1) % count, i) for i in range(ends)]),
            ],
            axis=dim,
        )
    return cells


def upwind(padded, courant_east, courant_north):
    center = padded[1:-1]
    south_row = padded[:-2]
    north_row = padded[2:]
    zero_column = jnp.zeros_like(center[:, :, :1])
    west_cell = jnp.concatenate([zero_column, center[:, :, :-1]], axis=2)
    east_cell = jnp.concatenate([center[:, :, 1:], zero_column], axis=2)
    return (
        center
        - jnp.maximum(courant_east, 0.0) * (center - west_cell)
        - jnp.minimum(courant_east, 0.0) * (east_cell - center)
        - jnp.maximum(courant_north, 0.0) * (center - south_row)
        - jnp.minimum(courant_north, 0.0) * (north_row - center)
    )


def source_update(cell_action, cell_mask, pattern, table):
    row_count = cell_action.shape[0]
    lane_count = cell_action.shape[2]
    group_size = 8
    offsets = (pattern - jnp.arange(ND, dtype=jnp.int32)[:, None]) % ND
    directions = jnp.arange(ND, dtype=jnp.int32)

    def advance_group(unused_state, group_rows):
        selector = (pattern[group_rows][:, :, None] == directions[None, None, :]).astype(
            jnp.float32
        )
        weights = table[offsets[group_rows]].astype(jnp.float32)
        assembled = jnp.einsum("rjc,rjab->racb", selector, weights)
        assembled = assembled.astype(jnp.bfloat16).reshape(group_size * NF, ND * NF)
        coupled = jnp.einsum(
            "ak,rkl->ral", assembled, cell_action, preferred_element_type=jnp.float32
        )
        return (unused_state, coupled)

    group_index = directions.reshape(ND // group_size, group_size)
    unused_state, coupled = lax.scan(advance_group, jnp.zeros((), jnp.float32), group_index)
    coupled = jnp.transpose(coupled, (1, 0, 2, 3)).reshape(row_count, ND * NF, lane_count)
    own_action = cell_action.astype(jnp.float32)
    sea_part = cell_mask.astype(jnp.float32)[:, None, :]
    result = own_action + sea_part * own_action * coupled
    return result.astype(jnp.bfloat16)


def local(action, east_current, north_current, sea_mask, pattern, table):
    tile_rows = action.shape[0]
    comp_count = action.shape[1]
    spec_count = lax.axis_size("spec")
    spec_index = lax.axis_index("spec")
    components = spec_index * comp_count + jnp.arange(comp_count, dtype=jnp.int32)
    direction = (components // NF).astype(jnp.float32)
    frequency = (components % NF).astype(jnp.float32)
    speed = jnp.exp(-2.0 * frequency / (NF - 1))
    theta = 2.0 * jnp.pi * direction / ND
    courant_east = courant_scale * (
        (speed * jnp.cos(theta))[None, :, None] + east_current[:, None, :]
    )
    courant_north = courant_scale * (
        (speed * jnp.sin(theta))[None, :, None] + north_current[:, None, :]
    )
    field = action.astype(jnp.float32)
    for substep in range(SUB):
        padded = extended(field, (("tile", 0),), 1)
        field = upwind(padded, courant_east, courant_north)
    moved = field.astype(jnp.bfloat16)
    share_rows = tile_rows // spec_count
    incoming = lax.all_to_all(moved, "spec", split_axis=0, concat_axis=1, tiled=True)
    own_mask = lax.dynamic_slice_in_dim(sea_mask, spec_index * share_rows, share_rows, 0)
    renewed = source_update(incoming, own_mask, pattern, table)
    result = lax.all_to_all(renewed, "spec", split_axis=1, concat_axis=0, tiled=True)
    return result


def solution(mesh):
    return jax.shard_map(
        local,
        mesh=mesh,
        in_specs=(
            P("tile", "spec", None),
            P("tile", None),
            P("tile", None),
            P("tile", None),
            P(),
            P(),
        ),
        out_specs=P("tile", "spec", None),
        check_vma=False,
    )
```

profile of v0, /device:TPU:0, one launch (start us, length us, event | category | flops | bytes accessed | tf_op | source)
XLA Modules:
  0.0 416.5 jit_solution(13679647613857830354)
XLA Ops:
  6.1 8.8 %convert_element_type.43 = f32[16,768,256]{2,1,0:T(8,128)} convert(bf16[16,768,256]{2,1,0:T(8,128)(2,1)} %param.8) | non-fusion elementwise | flops 3145728 | bytes 18874368 | tf_op jit(solution)/shard_map/convert_element_type | solution.py:91
  15.0 13.7 %fusion.39 = (f32[16,768,255]{2,1,0:T(8,128)}, f32[16,768,255]{2,1,0:T(8,128)}) fusion(bf16[16,768,256]{2,1,0:T(8,128)(2,1)} %param.8), kind=kLoop, calls=%fused_computation.73 | loop fusion | bytes 50135040 | tf_op jit(solution)/shard_map/slice | solution.py:36
  28.8 21.8 %fusion.10 = f32[16,768,256]{2,1,0:T(8,128)} fusion(bf16[16,768,256]{2,1,0:T(8,128)(2,1)S(1)} %bitcast.59, f32[1,768,256]{2,1,0:T(8,128)} %collective-permute-done.1, f32[16,768,256]{2,1,0:T(8,128)} %convert_element_type.43, f32[1,768,256]{2,1,0:T(8,128)S(1)} %collective-permute-done, f32[16,768,255]{2,1,0:T(8,128)} %get-tuple-element.104, ...), kind=kLoop, calls=%fused_computation.25 | loop fusion | flops 72351744 | bytes 58136576 | tf_op jit(solution)/shard_map/sub | solution.py:39
  58.9 20.6 %fusion.37 = (f32[16,768,255]{2,1,0:T(8,128)}, f32[16,768,255]{2,1,0:T(8,128)}) fusion(f32[16,768,256]{2,1,0:T(8,128)} %fusion.10), kind=kLoop, calls=%fused_computation.71 | loop fusion | bytes 50135040 | tf_op jit(solution)/shard_map/slice | solution.py:36
  79.6 15.7 %fusion.19 = bf16[16,768,256]{2,1,0:T(8,128)(2,1)} fusion(f32[16,768,256]{2,1,0:T(8,128)S(1)} %bitcast.61, f32[1,768,256]{2,1,0:T(8,128)S(1)} %collective-permute-done.3, f32[1,768,256]{2,1,0:T(8,128)S(1)} %collective-permute-done.2, f32[16,768,255]{2,1,0:T(8,128)} %get-tuple-element.100, f32[16,768,255]{2,1,0:T(8,128)} %get-tuple-element.99, ...), kind=kLoop, calls=%fused_computation.35 | loop fusion | flops 72351744 | bytes 45553664 | tf_op jit(solution)/shard_map/convert_element_type | solution.py:95
  95.3 5.6 %all-to-all-start = ((bf16[16,768,256]{2,1,0:T(8,128)(2,1)}), bf16[16,768,256]{2,1,0:T(8,128)(2,1)}, u32[]{:S(2)}, u32[]{:S(2)}) async-start(bf16[16,768,256]{2,1,0:T(8,128)(2,1)} %fusion.19), calls=%async_computation | async-start | bytes 12582912 | tf_op jit(solution)/shard_map/all_to_all | solution.py:97
  101.7 69.2 %all-to-all-done = bf16[16,768,256]{2,1,0:T(8,128)(2,1)} async-done(((bf16[16,768,256]{2,1,0:T(8,128)(2,1)}), bf16[16,768,256]{2,1,0:T(8,128)(2,1)}, u32[]{:S(2)}, u32[]{:S(2)}) %all-to-all-start) | async-done | bytes 6291488 | tf_op jit(solution)/shard_map/all_to_all | solution.py:97
  170.9 6.0 %copy.19 = bf16[4,4,768,256]{3,2,0,1:T(8,128)(2,1)} copy(bf16[4,4,768,256]{3,2,1,0:T(8,128)(2,1)} %bitcast) | data formatting | bytes 12582912 | tf_op jit(solution)/shard_map/all_to_all | solution.py:97
  177.0 142.8 %while.11 = (s32[]{:T(128)}, f32[6,4,512,256]{3,2,0,1:T(8,128)}, s32[6,8]{1,0:T(8,128)S(1)}, s32[48,24]{1,0:T(8,128)S(1)}, bf16[48,64,64]{2,1,0:T(8,128)(2,1)}, ...) while((s32[]{:T(128)}, f32[6,4,512,256]{3,2,0,1:T(8,128)}, ...), condition=%wide.region_1.2_spmd.clone, body=%wide.region_0.1_spmd.clone.sunk | while | flops 3298307584 | bytes 25707512 | solution.py:67
  185.7 7.5 %reshape.160 = bf16[512,3072,1]{1,0,2:T(8,128)(2,1)S(1)} reshape(bf16[8,64,48,64]{3,2,1,0:T(8,128)(2,1)} %convert_bitcast_fusion.2) | data formatting | bytes 6291456 | tf_op jit(solution)/shard_map/while/body/eval_jaxpr/reshape | solution.py:60
  193.3 7.6 %bitcast_dynamic-update-slice_fusion.2 = f32[6,4,512,256]{3,2,0,1:T(8,128)} fusion(f32[6,4,512,256]{3,2,0,1:T(8,128)} %get-tuple-element.161, s32[]{:T(128)} %get-tuple-element.160, bf16[512,3072,1]{1,0,2:T(8,128)(2,1)S(1)} %reshape.160, bf16[4,3072,256]{2,1,0:T(8,128)(2,1)} %get-tuple-element.174), kind=kOutput, calls=%fused_computation.6.clone.1 | convolution fusion | flops 3221225472 | bytes 11534848 | tf_op jit(solution)/shard_map/while/body/eval_jaxpr/ak,rkl->ral/dot_general | solution.py:61
  209.6 7.5 %reshape.160 = bf16[512,3072,1]{1,0,2:T(8,128)(2,1)S(1)} reshape(bf16[8,64,48,64]{3,2,1,0:T(8,128)(2,1)} %convert_bitcast_fusion.2) | data formatting | bytes 6291456 | tf_op jit(solution)/shard_map/while/body/eval_jaxpr/reshape | solution.py:60
  217.1 7.5 %bitcast_dynamic-update-slice_fusion.2 = f32[6,4,512,256]{3,2,0,1:T(8,128)} fusion(f32[6,4,512,256]{3,2,0,1:T(8,128)} %get-tuple-element.161, s32[]{:T(128)} %get-tuple-element.160, bf16[512,3072,1]{1,0,2:T(8,128)(2,1)S(1)} %reshape.160, bf16[4,3072,256]{2,1,0:T(8,128)(2,1)} %get-tuple-element.174), kind=kOutput, calls=%fused_computation.6.clone.1 | convolution fusion | flops 3221225472 | bytes 11534848 | tf_op jit(solution)/shard_map/while/body/eval_jaxpr/ak,rkl->ral/dot_general | solution.py:61
  233.4 7.5 %reshape.160 = bf16[512,3072,1]{1,0,2:T(8,128)(2,1)S(1)} reshape(bf16[8,64,48,64]{3,2,1,0:T(8,128)(2,1)} %convert_bitcast_fusion.2) | data formatting | bytes 6291456 | tf_op jit(solution)/shard_map/while/body/eval_jaxpr/reshape | solution.py:60
  240.9 7.6 %bitcast_dynamic-update-slice_fusion.2 = f32[6,4,512,256]{3,2,0,1:T(8,128)} fusion(f32[6,4,512,256]{3,2,0,1:T(8,128)} %get-tuple-element.161, s32[]{:T(128)} %get-tuple-element.160, bf16[512,3072,1]{1,0,2:T(8,128)(2,1)S(1)} %reshape.160, bf16[4,3072,256]{2,1,0:T(8,128)(2,1)} %get-tuple-element.174), kind=kOutput, calls=%fused_computation.6.clone.1 | convolution fusion | flops 3221225472 | bytes 11534848 | tf_op jit(solution)/shard_map/while/body/eval_jaxpr/ak,rkl->ral/dot_general | solution.py:61
  257.2 7.5 %reshape.160 = bf16[512,3072,1]{1,0,2:T(8,128)(2,1)S(1)} reshape(bf16[8,64,48,64]{3,2,1,0:T(8,128)(2,1)} %convert_bitcast_fusion.2) | data formatting | bytes 6291456 | tf_op jit(solution)/shard_map/while/body/eval_jaxpr/reshape | solution.py:60
  264.7 7.5 %bitcast_dynamic-update-slice_fusion.2 = f32[6,4,512,256]{3,2,0,1:T(8,128)} fusion(f32[6,4,512,256]{3,2,0,1:T(8,128)} %get-tuple-element.161, s32[]{:T(128)} %get-tuple-element.160, bf16[512,3072,1]{1,0,2:T(8,128)(2,1)S(1)} %reshape.160, bf16[4,3072,256]{2,1,0:T(8,128)(2,1)} %get-tuple-element.174), kind=kOutput, calls=%fused_computation.6.clone.1 | convolution fusion | flops 3221225472 | bytes 11534848 | tf_op jit(solution)/shard_map/while/body/eval_jaxpr/ak,rkl->ral/dot_general | solution.py:61
  280.9 7.5 %reshape.160 = bf16[512,3072,1]{1,0,2:T(8,128)(2,1)S(1)} reshape(bf16[8,64,48,64]{3,2,1,0:T(8,128)(2,1)} %convert_bitcast_fusion.2) | data formatting | bytes 6291456 | tf_op jit(solution)/shard_map/while/body/eval_jaxpr/reshape | solution.py:60
  288.5 7.5 %bitcast_dynamic-update-slice_fusion.2 = f32[6,4,512,256]{3,2,0,1:T(8,128)} fusion(f32[6,4,512,256]{3,2,0,1:T(8,128)} %get-tuple-element.161, s32[]{:T(128)} %get-tuple-element.160, bf16[512,3072,1]{1,0,2:T(8,128)(2,1)S(1)} %reshape.160, bf16[4,3072,256]{2,1,0:T(8,128)(2,1)} %get-tuple-element.174), kind=kOutput, calls=%fused_computation.6.clone.1 | convolution fusion | flops 3221225472 | bytes 11534848 | tf_op jit(solution)/shard_map/while/body/eval_jaxpr/ak,rkl->ral/dot_general | solution.py:61
  304.7 7.5 %reshape.160 = bf16[512,3072,1]{1,0,2:T(8,128)(2,1)S(1)} reshape(bf16[8,64,48,64]{3,2,1,0:T(8,128)(2,1)} %convert_bitcast_fusion.2) | data formatting | bytes 6291456 | tf_op jit(solution)/shard_map/while/body/eval_jaxpr/reshape | solution.py:60
  312.2 7.5 %bitcast_dynamic-update-slice_fusion.2 = f32[6,4,512,256]{3,2,0,1:T(8,128)} fusion(f32[6,4,512,256]{3,2,0,1:T(8,128)} %get-tuple-element.161, s32[]{:T(128)} %get-tuple-element.160, bf16[512,3072,1]{1,0,2:T(8,128)(2,1)S(1)} %reshape.160, bf16[4,3072,256]{2,1,0:T(8,128)(2,1)} %get-tuple-element.174), kind=kOutput, calls=%fused_computation.6.clone.1 | convolution fusion | flops 3221225472 | bytes 11534848 | tf_op jit(solution)/shard_map/while/body/eval_jaxpr/ak,rkl->ral/dot_general | solution.py:61
  319.8 10.8 %fusion.15 = bf16[4,3072,256]{2,1,0:T(8,128)(2,1)} fusion(f32[6,4,512,256]{3,2,0,1:T(8,128)} %get-tuple-element.47, f32[4,256]{1,0:T(4,128)S(1)} %dynamic-slice_convert_fusion, bf16[4,4,768,256]{3,2,0,1:T(8,128)(2,1)} %bitcast.64), kind=kLoop, calls=%fused_computation.30 | loop fusion | flops 15728640 | bytes 25169920 | tf_op jit(solution)/shard_map/convert_element_type | solution.py:72
  330.6 8.1 %copy.23 = bf16[4,3072,256]{2,0,1:T(4,128)(2,1)S(1)} copy(bf16[4,3072,256]{2,1,0:T(8,128)(2,1)} %fusion.15) | data formatting | bytes 12582912 | tf_op jit(solution)/shard_map/convert_element_type | solution.py:72
  338.7 74.0 %all_to_all.36 = bf16[4,3072,256]{2,0,1:T(4,128)(2,1)S(1)} all-to-all(bf16[4,3072,256]{2,0,1:T(4,128)(2,1)S(1)} %copy.23), channel_id=1, replica_groups=mesh['spec'=4,'tile'=8] {'spec'}, dimensions={1} | all-to-all | bytes 12582912 | tf_op jit(solution)/shard_map/all_to_all | solution.py:100
  (89 shorter events, 71.4 us)
Async XLA Ops:
  2.4 26.3 %collective-permute-start = (f32[1,768,256]{2,1,0:T(8,128)}, f32[1,768,256]{2,1,0:T(8,128)S(1)}, u32[]{:S(2)}, u32[]{:S(2)}) collective-permute-start(f32[1,768,256]{2,1,0:T(8,128)} %get-tuple-element.105), channel_id=1, source_target_pairs={{0,1},{1,2},{2,3},{3,4},{4,5},{5,6},{6,7},{8,9},{9,10},{10,11},{11... | collective-permute-start | bytes 2359304 | tf_op jit(solution)/shard_map/ppermute | solution.py:22
  4.8 23.9 %collective-permute-start.1 = (f32[1,768,256]{2,1,0:T(8,128)}, f32[1,768,256]{2,1,0:T(8,128)}, u32[]{:S(2)}, u32[]{:S(2)}) collective-permute-start(f32[1,768,256]{2,1,0:T(8,128)} %get-tuple-element.106), channel_id=1, source_target_pairs={{1,0},{2,1},{3,2},{4,3},{5,4},{6,5},{7,6},{9,8},{10,9},{11,10},{12... | collective-permute-start | bytes 2359304 | tf_op jit(solution)/shard_map/ppermute | solution.py:24
  6.1 22.6 %slice-start = ((s8[6291456]{0:T(1024)(128)(4,1)}), s8[2097152]{0:T(1024)(128)(4,1)S(1)}, s32[]{:S(2)}) async-start(s8[6291456]{0:T(1024)(128)(4,1)} %bitcast.58), calls=%async_computation.2 | async-start | bytes 4194304
  14.9 13.8 %slice-start.1 = ((s8[6291456]{0:T(1024)(128)(4,1)}), s8[4194304]{0:T(1024)(128)(4,1)S(1)}, s32[]{:S(2)}) async-start(s8[6291456]{0:T(1024)(128)(4,1)} %bitcast.58), calls=%async_computation.3 | async-start | bytes 8388608
  15.0 13.8 %copy-start = (f32[16,256]{1,0:T(8,128)S(1)}, f32[16,256]{1,0:T(8,128)}, u32[]{:S(2)}) copy-start(f32[16,256]{1,0:T(8,128)} %param.10) | copy-start | bytes 49156
  15.0 13.8 %copy-start.1 = (f32[16,256]{1,0:T(8,128)S(1)}, f32[16,256]{1,0:T(8,128)}, u32[]{:S(2)}) copy-start(f32[16,256]{1,0:T(8,128)} %param.9) | copy-start | bytes 49156
  52.1 27.5 %collective-permute-start.2 = (f32[1,768,256]{2,1,0:T(8,128)S(1)}, f32[1,768,256]{2,1,0:T(8,128)S(1)}, u32[]{:S(2)}, u32[]{:S(2)}) collective-permute-start(f32[1,768,256]{2,1,0:T(8,128)S(1)} %get-tuple-element.101), channel_id=1, source_target_pairs={{0,1},{1,2},{2,3},{3,4},{4,5},{5,6},{6,7},{8,9},{9,10},{10,11},{11... | collective-permute-start | bytes 2359304 | tf_op jit(solution)/shard_map/ppermute | solution.py:22
  57.3 22.2 %slice-start.2 = ((s8[12582912]{0:T(1024)(128)(4,1)}), s8[4194304]{0:T(1024)(128)(4,1)S(1)}, s32[]{:S(2)}) async-start(s8[12582912]{0:T(1024)(128)(4,1)} %bitcast.60), calls=%async_computation.4 | async-start | bytes 8388608
  57.3 22.2 %slice-start.3 = ((s8[12582912]{0:T(1024)(128)(4,1)}), s8[4194304]{0:T(1024)(128)(4,1)S(1)}, s32[]{:S(2)}) async-start(s8[12582912]{0:T(1024)(128)(4,1)} %bitcast.60), calls=%async_computation.5 | async-start | bytes 8388608
  57.3 22.2 %slice-start.4 = ((s8[12582912]{0:T(1024)(128)(4,1)}), s8[4194304]{0:T(1024)(128)(4,1)S(1)}, s32[]{:S(2)}) async-start(s8[12582912]{0:T(1024)(128)(4,1)} %bitcast.60), calls=%async_computation.6 | async-start | bytes 8388608
  57.3 22.2 %collective-permute-start.3 = (f32[1,768,256]{2,1,0:T(8,128)S(1)}, f32[1,768,256]{2,1,0:T(8,128)S(1)}, u32[]{:S(2)}, u32[]{:S(2)}) collective-permute-start(f32[1,768,256]{2,1,0:T(8,128)S(1)} %get-tuple-element.102), channel_id=1, source_target_pairs={{1,0},{2,1},{3,2},{4,3},{5,4},{6,5},{7,6},{9,8},{10,9},{11,10},{12... | collective-permute-start | bytes 2359304 | tf_op jit(solution)/shard_map/ppermute | solution.py:24
  95.3 5.6 %copy-start.2 = (s32[48,24]{0,1:T(8,128)S(1)}, s32[48,24]{0,1:T(8,128)}, u32[]{:S(2)}) copy-start(s32[48,24]{0,1:T(8,128)} %param.12) | copy-start | bytes 13828
  95.3 75.6 %all-to-all-start = ((bf16[16,768,256]{2,1,0:T(8,128)(2,1)}), bf16[16,768,256]{2,1,0:T(8,128)(2,1)}, u32[]{:S(2)}, u32[]{:S(2)}) async-start(bf16[16,768,256]{2,1,0:T(8,128)(2,1)} %fusion.19), calls=%async_computation | async-start | bytes 12582912 | tf_op jit(solution)/shard_map/all_to_all | solution.py:97
where the time goes:
time: 418 us; the launch traced here: 417 us
  local copies, waits for them, and re-layouts  122 us (29%)
  matrix products  76.5 us (18%)
  blocking collectives  74 us (18%)
  waiting for transfers between devices  69.2 us (17%)
  other arithmetic  58.1 us (14%)
  starting transfers between devices  16 us (4%)
    all_to_all x1, blocking collectives, local(): lax.all_to_all(renewed, 'spec', split_axis=1, concat_axis=0, tiled=True)  74 us
    all_to_all x1, waiting for transfers between devices, local(): lax.all_to_all(moved, 'spec', split_axis=0, concat_axis=1, tiled=True)  69.2 us
    dot_general x6, matrix products, advance_group(): jnp.einsum('ak,rkl->ral', assembled, cell_action, preferred_element_type=...  45.2 us
    reshape x6, local copies, waits for them, and re-layouts, advance_group(): assembled = assembled.astype(jnp.bfloat16).reshape(group_size * NF, ND * NF)  45 us
    slice x2, local copies, waits for them, and re-layouts, upwind(): west_cell = jnp.concatenate([zero_column, center[:, :, :-1]], axis=2)  34.4 us
    dot_general x6, matrix products, advance_group(): assembled = jnp.einsum('rjc,rjab->racb', selector, weights)  31.3 us
    sub x1, other arithmetic, upwind(): center - jnp.maximum(courant_east, 0.0) * (center - west_cell)  21.8 us
    gather x12, local copies, waits for them, and re-layouts, advance_group(): weights = table[offsets[group_rows]].astype(jnp.float32)  17.1 us
  transfers between devices with their start and end apart: 5, of which 1 were waited for; matrix products, arithmetic and copies ran while one was open for 11% of the time, Pallas kernels for 0%

commit v1 on v0

v1 whole, which is shorter than its diff:
```python
import functools

import jax
import jax.numpy as jnp
from jax import lax
from jax.experimental import pallas as pl
from jax.experimental.pallas import tpu as pltpu
from jax.sharding import PartitionSpec as P

NF = 64
ND = 48
SEA = 2048
WINDOW = 512
STEP = 256
SUBK = 16
courant_scale = 0.45
VMEM_LIMIT = 48 * 1024 * 1024


def split_directions(count, sizes):
    if sum(sizes) == count:
        return sizes
    return (1,) * count


def offsets_of(sizes):
    return [sum(sizes[:i]) for i in range(len(sizes))]


def propagate_kernel(rows, peers, share, meta, act, low, high, ae_ref, an_ref, be_ref, bn_ref, slot_t, *rest):
    moved = rest[-(peers + 3)]
    outs = rest[-(peers + 2):-2]
    onehot, packed = rest[-2:]
    lon = act.shape[2]
    depth = act.shape[1]

    @pl.when(pl.program_id(0) == 0)
    def build():
        lanes = lax.broadcasted_iota(jnp.int32, (lon, WINDOW), 1)
        for r in range(rows):
            hit = (slot_t[:, r:r + 1] - meta[3 + r]) == lanes
            onehot[r] = jnp.where(hit, 1.0, 0.0).astype(jnp.bfloat16)

    lane = lax.broadcasted_iota(jnp.int32, (SUBK, lon), 1)
    first = lane == 0
    last = lane == lon - 1

    def group(i, carry):
        ks = pl.ds(pl.multiple_of(i * SUBK, SUBK), SUBK)
        ae = jnp.concatenate([ae_ref[ks, :]] * (lon // 128), axis=1)
        an = jnp.concatenate([an_ref[ks, :]] * (lon // 128), axis=1)

        def load(r):
            if r < 0:
                block = low[r + 2, ks, :]
            elif r < rows:
                block = act[r, ks, :]
            else:
                block = high[r - rows, ks, :]
            return block.astype(jnp.float32)

        def advance(center, south, north, ce, cn):
            west = jnp.where(first, 0.0, pltpu.roll(center, 1, 1))
            east = jnp.where(last, 0.0, pltpu.roll(center, lon - 1, 1))
            along = jnp.where(ce > 0.0, west, east)
            across = jnp.where(cn > 0.0, south, north)
            return center - jnp.abs(ce) * (center - along) - jnp.abs(cn) * (center - across)

        below, here = load(-2), load(-1)
        once = {}
        courant = {}
        for r in range(-1, rows + 1):
            above = load(r + 1)
            ce = ae + be_ref[r + 1:r + 2, :]
            cn = an + bn_ref[r + 1:r + 2, :]
            value = advance(here, below, above, ce, cn)
            if r == -1:
                value = jnp.where(meta[1] > 0, value, 0.0)
            if r == rows:
                value = jnp.where(meta[2] > 0, value, 0.0)
            once[r] = value
            courant[r] = (ce, cn)
            if r >= 1:
                twice = advance(once[r - 1], once[r - 2], once[r], *courant[r - 1])
                moved[r - 1, ks, :] = twice.astype(jnp.bfloat16)
            below, here = here, above
        return carry

    lax.fori_loop(0, depth // SUBK, group, 0)

    packed[...] = jnp.zeros_like(packed)
    for r in range(rows):
        window = pl.ds(pl.multiple_of(meta[3 + r], STEP), WINDOW)
        part = jnp.dot(moved[r], onehot[r], preferred_element_type=jnp.float32)
        packed[:, window] += part.astype(jnp.bfloat16)
    me = meta[0]
    for k in range(peers):
        start = pl.multiple_of((me ^ k) * share, 128)
        outs[k][...] = packed[:, pl.ds(start, share)]


def propagate(meta, action, low, high, ae, an, be, bn, slot_t, moved, begin, count, peers):
    rows, comps, lon = action.shape
    share = SEA // peers
    here = lambda s, m: (0, begin + s, 0)
    local = lambda s, m: (0, s, 0)
    flat = lambda s, m: (begin + s, 0)
    whole = lambda s, m: (0, 0)
    in_specs = [
        pl.BlockSpec((rows, NF, lon), here),
        pl.BlockSpec((2, NF, lon), local),
        pl.BlockSpec((2, NF, lon), local),
        pl.BlockSpec((NF, 128), flat),
        pl.BlockSpec((NF, 128), flat),
        pl.BlockSpec((rows + 2, lon), whole),
        pl.BlockSpec((rows + 2, lon), whole),
        pl.BlockSpec((lon, rows), whole),
    ]
    args = [meta, action, low, high, ae, an, be, bn, slot_t]
    aliases = {}
    if moved is not None:
        in_specs.append(pl.BlockSpec(memory_space=pl.ANY))
        aliases = {len(args): 0}
        args.append(moved)
    cells = count * NF * rows * lon
    return pl.pallas_call(
        functools.partial(propagate_kernel, rows, peers, share),
        grid_spec=pltpu.PrefetchScalarGridSpec(
            num_scalar_prefetch=1,
            grid=(count,),
            in_specs=in_specs,
            out_specs=[pl.BlockSpec((rows, NF, lon), here)]
            + [pl.BlockSpec((NF, share), lambda s, m: (s, 0))] * peers,
            scratch_shapes=[
                pltpu.VMEM((rows, lon, WINDOW), jnp.bfloat16),
                pltpu.VMEM((NF, SEA), jnp.bfloat16),
            ],
        ),
        out_shape=[jax.ShapeDtypeStruct(action.shape, jnp.bfloat16)]
        + [jax.ShapeDtypeStruct((count * NF, share), jnp.bfloat16)] * peers,
        input_output_aliases=aliases,
        compiler_params=pltpu.CompilerParams(vmem_limit_bytes=VMEM_LIMIT),
        cost_estimate=pl.CostEstimate(
            flops=cells * 2 * WINDOW, bytes_accessed=cells * 6, transcendentals=0
        ),
        name="propagate",
    )(*args)


def couple_kernel(peers, dirs, begin, size, spots, meta, sel, tt, *rest):
    pieces = rest[:len(spots)]
    outs = rest[len(spots):len(spots) + peers]
    x, w, y, in_sem, out_sem = rest[len(spots) + peers:]
    me = meta[0]
    copies = []
    for i, (k, first) in enumerate(spots):
        depth = pieces[i].shape[0]
        start = pl.multiple_of(((me ^ k) * dirs + first) * NF, NF)
        copies.append(pltpu.make_async_copy(pieces[i], x.at[pl.ds(start, depth), :], in_sem.at[i]))
        copies[-1].start()
    for copy in copies:
        copy.wait()

    def peer(p, carry):
        for d in range(size):
            r = p * dirs + begin + d
            turn = lax.rem(ND - r, ND)
            lanes = pl.ds(pl.multiple_of((turn // 2) * 128, 128), ND * NF)
            keep = jnp.broadcast_to(sel[pl.ds(r, 1), :], (16, ND * NF)).astype(jnp.bfloat16)
            for q in range(NF // 16):
                w[pl.ds(d * NF + q * 16, 16), :] = tt[turn % 2, pl.ds(q * 16, 16), lanes] * keep
        coupled = jnp.dot(w[...], x[...], preferred_element_type=jnp.float32)
        own = x[pl.ds(pl.multiple_of((p * dirs + begin) * NF, NF), size * NF), :].astype(jnp.float32)
        y[p] = (own + own * coupled).astype(jnp.bfloat16)
        return carry

    lax.fori_loop(0, peers, peer, 0)
    copies = []
    for k in range(peers):
        copies.append(pltpu.make_async_copy(y.at[me ^ k], outs[k], out_sem.at[k]))
        copies[-1].start()
    for copy in copies:
        copy.wait()


def couple(meta, sel, tt, pieces, spots, begin, size, peers, dirs):
    share = SEA // peers
    return pl.pallas_call(
        functools.partial(couple_kernel, peers, dirs, begin, size, spots),
        in_specs=[
            pl.BlockSpec(memory_space=pltpu.SMEM),
            pl.BlockSpec(memory_space=pltpu.VMEM),
            pl.BlockSpec(memory_space=pltpu.VMEM),
        ]
        + [pl.BlockSpec(memory_space=pl.ANY)] * len(pieces),
        out_specs=[pl.BlockSpec(memory_space=pl.ANY)] * peers,
        out_shape=[jax.ShapeDtypeStruct((size * NF, share), jnp.bfloat16)] * peers,
        scratch_shapes=[
            pltpu.VMEM((ND * NF, share), jnp.bfloat16),
            pltpu.VMEM((size * NF, ND * NF), jnp.bfloat16),
            pltpu.VMEM((peers, size * NF, share), jnp.bfloat16),
            pltpu.SemaphoreType.DMA((len(pieces),)),
            pltpu.SemaphoreType.DMA((peers,)),
        ],
        compiler_params=pltpu.CompilerParams(vmem_limit_bytes=VMEM_LIMIT),
        cost_estimate=pl.CostEstimate(
            flops=2 * peers * size * NF * ND * NF * share,
            bytes_accessed=2 * (ND * NF + peers * size * NF) * share,
            transcendentals=0,
        ),
        name="couple",
    )(meta, sel, tt, *pieces)


def finish_kernel(peers, share, group, meta, slot, moved, *rest):
    pieces = rest[:peers]
    out, renewed, sem = rest[peers:]
    me = meta[0]

    @pl.when(pl.program_id(0) == 0)
    def fetch():
        copies = []
        for k in range(peers):
            start = pl.multiple_of((me ^ k) * share, 128)
            copies.append(pltpu.make_async_copy(pieces[k], renewed.at[:, pl.ds(start, share)], sem.at[k]))
            copies[-1].start()
        for copy in copies:
            copy.wait()

    lon = moved.shape[2]
    spots = lax.broadcasted_iota(jnp.int32, (WINDOW, lon), 0)
    for i in range(group):
        r = pl.program_id(0) * group + i
        base = pl.multiple_of(meta[3 + r], STEP)
        cells = slot[pl.ds(r, 1), :]
        hit = (cells - base) == spots
        onehot = jnp.where(hit, 1.0, 0.0).astype(jnp.bfloat16)
        spread = jnp.dot(renewed[:, pl.ds(base, WINDOW)], onehot, preferred_element_type=jnp.float32)
        out[i] = jnp.where(cells >= 0, spread, moved[i].astype(jnp.float32)).astype(jnp.bfloat16)


def finish(meta, slot, moved, pieces, which, size, peers):
    rows, comps, lon = moved.shape
    share = SEA // peers
    group = 4
    block = pl.BlockSpec((group, size * NF, lon), lambda s, m: (s, which, 0))
    return pl.pallas_call(
        functools.partial(finish_kernel, peers, share, group),
        grid_spec=pltpu.PrefetchScalarGridSpec(
            num_scalar_prefetch=1,
            grid=(rows // group,),
            in_specs=[pl.BlockSpec((rows, lon), lambda s, m: (0, 0)), block]
            + [pl.BlockSpec(memory_space=pl.ANY)] * peers,
            out_specs=block,
            scratch_shapes=[
                pltpu.VMEM((size * NF, SEA), jnp.bfloat16),
                pltpu.SemaphoreType.DMA((peers,)),
            ],
        ),
        out_shape=jax.ShapeDtypeStruct(moved.shape, jnp.bfloat16),
        input_output_aliases={2: 0},
        compiler_params=pltpu.CompilerParams(vmem_limit_bytes=VMEM_LIMIT),
        cost_estimate=pl.CostEstimate(
            flops=2 * rows * size * NF * lon * WINDOW,
            bytes_accessed=4 * rows * size * NF * lon,
            transcendentals=0,
        ),
        name="finish",
    )(meta, slot, moved, *pieces)


def pass_on(array, axis, up):
    count = lax.axis_size(axis)
    if up:
        return lax.ppermute(array, axis, [(i, i + 1) for i in range(count - 1)])
    return lax.ppermute(array, axis, [(i + 1, i) for i in range(count - 1)])


def local(action, east_current, north_current, sea_mask, pattern, table):
    rows, comps, lon = action.shape
    peers = lax.axis_size("spec")
    me = lax.axis_index("spec")
    tile = lax.axis_index("tile")
    tiles = lax.axis_size("tile")
    dirs = comps // NF
    parts_out = split_directions(dirs, (1, 2, 3, 6))
    parts_back = split_directions(dirs, (3, 3, 3, 3))

    currents = jnp.stack([east_current, north_current]) * courant_scale
    low_current = pass_on(currents[:, rows - 1:, :], "tile", True)
    high_current = pass_on(currents[:, :1, :], "tile", False)
    halos = []
    for begin, count in zip(offsets_of(parts_out), parts_out):
        part = slice(begin * NF, (begin + count) * NF)
        halos.append((
            pass_on(action[rows - 2:, part, :], "tile", True),
            pass_on(action[:2, part, :], "tile", False),
        ))
    wide = jnp.concatenate([low_current, currents, high_current], axis=1)
    be, bn = wide[0], wide[1]

    components = me * comps + jnp.arange(comps, dtype=jnp.int32)
    direction = (components // NF).astype(jnp.float32)
    frequency = (components % NF).astype(jnp.float32)
    speed = courant_scale * jnp.exp(-2.0 * frequency / (NF - 1))
    theta = 2.0 * jnp.pi * direction / ND
    ae = jnp.broadcast_to((speed * jnp.cos(theta))[:, None], (comps, 128))
    an = jnp.broadcast_to((speed * jnp.sin(theta))[:, None], (comps, 128))

    sea = sea_mask > 0
    before = jnp.dot(
        sea.astype(jnp.bfloat16),
        jnp.triu(jnp.ones((lon, lon), jnp.bfloat16), 1),
        preferred_element_type=jnp.float32,
    )
    totals = jnp.sum(sea.astype(jnp.float32), axis=1)
    starts = jnp.sum(
        jnp.where(jnp.tril(jnp.ones((rows, rows), jnp.bool_), -1), totals[None, :], 0.0), axis=1
    )
    slot = jnp.where(sea, (before + starts[:, None]).astype(jnp.int32), -1)
    bases = jnp.minimum(starts.astype(jnp.int32) // STEP * STEP, SEA - WINDOW)
    meta = jnp.concatenate([
        jnp.stack([me, (tile > 0).astype(jnp.int32), (tile < tiles - 1).astype(jnp.int32)]),
        bases,
    ]).astype(jnp.int32)
    slot_t = slot.T

    chosen = jnp.any(pattern[:, :, None] == jnp.arange(ND, dtype=jnp.int32), axis=1)
    sel = jnp.repeat(chosen.astype(jnp.float32), NF, axis=1)
    flat = jnp.transpose(table, (1, 0, 2)).reshape(NF, ND * NF)
    twofold = jnp.concatenate([flat, flat], axis=1)
    tt = jnp.stack([twofold, jnp.roll(twofold, -NF, axis=1)])

    moved = None
    pieces, spots = [], []
    for j, (begin, count) in enumerate(zip(offsets_of(parts_out), parts_out)):
        low, high = halos[j]
        moved, *packed = propagate(
            meta, action, low, high, ae, an, be, bn, slot_t, moved, begin, count, peers
        )
        for k in range(peers):
            piece = packed[k]
            if k:
                piece = lax.ppermute(piece, "spec", [(i, i ^ k) for i in range(peers)])
            pieces.append(piece)
            spots.append((k, begin))

    result = moved
    for g, (begin, size) in enumerate(zip(offsets_of(parts_back), parts_back)):
        renewed = couple(meta, sel, tt, pieces, tuple(spots), begin, size, peers, dirs)
        back = [renewed[0]] + [
            lax.ppermute(renewed[k], "spec", [(i, i ^ k) for i in range(peers)])
            for k in range(1, peers)
        ]
        result = finish(meta, slot, result, back, begin // size, size, peers)
    return result


def solution(mesh):
    return jax.shard_map(
        local,
        mesh=mesh,
        in_specs=(
            P("tile", "spec", None),
            P("tile", None),
            P("tile", None),
            P("tile", None),
            P(),
            P(),
        ),
        out_specs=P("tile", "spec", None),
        check_vma=False,
    )
```

time: 418 us -> 202 us (0.48)
  Pallas kernels: 0 us -> 104 us
  local copies, waits for them, and re-layouts: 122 us -> 21.4 us
  matrix products: 76.5 us -> 0.11 us
  blocking collectives: 74 us -> 0 us
  other arithmetic: 58.1 us -> 2.45 us
  waiting for transfers between devices: 69.2 us -> 16.8 us
  starting transfers between devices: 16 us -> 55.6 us
    pallas_call x0 -> x12, Pallas kernels: none -> 104 us  [the longest x4 50.1 us: propagate(): pl.pallas_call(functools.partial(propagate_kernel, rows, peers, share), g...]
    dot_general x12 -> x1, matrix products: 76.5 us -> 0.11 us  [local(): jnp.dot(sea.astype(jnp.bfloat16), jnp.triu(jnp.ones((lon, lon), jnp.bfloa...]
    all_to_all x1 -> x0, blocking collectives: 74 us -> none  [local(): lax.all_to_all(renewed, 'spec', split_axis=1, concat_axis=0, tiled=True)]
    all_to_all x1 -> x0, waiting for transfers between devices: 69.2 us -> none  [local(): lax.all_to_all(moved, 'spec', split_axis=0, concat_axis=1, tiled=True)]
    ppermute x4 -> x34, starting transfers between devices: 10.5 us -> 55.6 us  [the longest x5 20.4 us: pass_on(): return lax.ppermute(array, axis, [(i, i + 1) for i in range(count - 1)])]
    reshape x6 -> x2, local copies, waits for them, and re-layouts: 45 us -> 2.13 us  [the longest x1 1.6 us: local(): sel = jnp.repeat(chosen.astype(jnp.float32), NF, axis=1)]
    convert_element_type x4 -> x1, other arithmetic: 36.1 us -> 0.01 us  [local(): sel = jnp.repeat(chosen.astype(jnp.float32), NF, axis=1)]
    slice x4 -> x8, local copies, waits for them, and re-layouts: 38.2 us -> 4.4 us  [the longest x4 4.11 us: local(): action[:2, part, :]]
  transfers between devices with their start and end apart: 5 -> 34, of which waited for: 1 -> 3; matrix products, arithmetic and copies ran while one was open for 11% -> 6% of each run, Pallas kernels for 0% -> 45%
where the time goes in v1:
time: 202 us; the launch traced here: 201 us
  Pallas kernels  104 us (51%)
  starting transfers between devices  55.6 us (28%)
  local copies, waits for them, and re-layouts  21.4 us (11%)
  waiting for transfers between devices  16.8 us (8%)
  other arithmetic  2.45 us (1%)
    pallas_call x4, Pallas kernels, propagate(): pl.pallas_call(functools.partial(propagate_kernel, rows, peers, share), g...  50.1 us
    pallas_call x4, Pallas kernels, couple(): pl.pallas_call(functools.partial(couple_kernel, peers, dirs, begin, size,...  33.5 us
    ppermute x5, starting transfers between devices, pass_on(): return lax.ppermute(array, axis, [(i, i + 1) for i in range(count - 1)])  20.4 us
    pallas_call x4, Pallas kernels, finish(): pl.pallas_call(functools.partial(finish_kernel, peers, share, group), gri...  20 us
    ppermute x12, waiting for transfers between devices, local(): piece = lax.ppermute(piece, 'spec', [(i, i ^ k) for i in range(peers)])  16.7 us
    ppermute x12, starting transfers between devices, local(): lax.ppermute(renewed[k], 'spec', [(i, i ^ k) for i in range(peers)])  14.3 us
    ppermute x12, starting transfers between devices, local(): piece = lax.ppermute(piece, 'spec', [(i, i ^ k) for i in range(peers)])  14.2 us
    unnamed x56, local copies, waits for them, and re-layouts  11.4 us
  transfers between devices with their start and end apart: 34, of which 3 were waited for; matrix products, arithmetic and copies ran while one was open for 6% of the time, Pallas kernels for 45%

profile of v1, /device:TPU:0, one launch (start us, length us, event | category | flops | bytes accessed | tf_op | source)
XLA Modules:
  0.0 200.7 jit_solution(12220519051817336377)
XLA Ops:
  0.7 2.4 %collective-permute-start.2 = (f32[2,1,256]{2,1,0:T(1,128)S(1)}, f32[2,1,256]{2,1,0:T(1,128)S(1)}, u32[]{:S(2)}, u32[]{:S(2)}) collective-permute-start(f32[2,1,256]{2,1,0:T(1,128)S(1)} %get-tuple-element.89), channel_id=1, source_target_pairs={{0,1},{1,2},{2,3},{3,4},{4,5},{5,6},{6,7},{8,9},{9,10},{10,11},{11... | collective-permute-start | bytes 6152 | tf_op jit(solution)/shard_map/ppermute | solution.py:275
  5.3 5.2 %collective-permute-start.8 = (bf16[2,64,256]{2,1,0:T(8,128)(2,1)S(1)}, bf16[2,64,256]{2,1,0:T(8,128)(2,1)S(1)}, u32[]{:S(2)}, u32[]{:S(2)}) collective-permute-start(bf16[2,64,256]{2,1,0:T(8,128)(2,1)S(1)} %get-tuple-element.80), channel_id=1, source_target_pairs={{0,1},{1,2},{2,3},{3,4},{4,5},{5,6},{6,7},{8,9},{9,10},{10,11},{11... | collective-permute-start | bytes 196616 | tf_op jit(solution)/shard_map/ppermute | solution.py:275
  12.8 4.3 %collective-permute-start.6 = (bf16[2,128,256]{2,1,0:T(8,128)(2,1)S(1)}, bf16[2,128,256]{2,1,0:T(8,128)(2,1)S(1)}, u32[]{:S(2)}, u32[]{:S(2)}) collective-permute-start(bf16[2,128,256]{2,1,0:T(8,128)(2,1)S(1)} %get-tuple-element.82), channel_id=1, source_target_pairs={{0,1},{1,2},{2,3},{3,4},{4,5},{5,6},{6,7},{8,9},{9,10},{10,11},{11... | collective-permute-start | bytes 393224 | tf_op jit(solution)/shard_map/ppermute | solution.py:275
  20.6 1.6 copy.25
  24.7 4.3 %collective-permute-start.4 = (bf16[2,192,256]{2,1,0:T(8,128)(2,1)S(1)}, bf16[2,192,256]{2,1,0:T(8,128)(2,1)S(1)}, u32[]{:S(2)}, u32[]{:S(2)}) collective-permute-start(bf16[2,192,256]{2,1,0:T(8,128)(2,1)S(1)} %get-tuple-element.84), channel_id=1, source_target_pairs={{0,1},{1,2},{2,3},{3,4},{4,5},{5,6},{6,7},{8,9},{9,10},{10,11},{11... | collective-permute-start | bytes 589832 | tf_op jit(solution)/shard_map/ppermute | solution.py:275
  30.3 4.3 %collective-permute-start = (bf16[2,384,256]{2,1,0:T(8,128)(2,1)S(1)}, bf16[2,384,256]{2,1,0:T(8,128)(2,1)S(1)}, u32[]{:S(2)}, u32[]{:S(2)}) collective-permute-start(bf16[2,384,256]{2,1,0:T(8,128)(2,1)S(1)} %get-tuple-element.86), channel_id=1, source_target_pairs={{0,1},{1,2},{2,3},{3,4},{4,5},{5,6},{6,7},{8,9},{9,10},{10,11},{11... | collective-permute-start | bytes 1179656 | tf_op jit(solution)/shard_map/ppermute | solution.py:275
  35.0 6.4 %propagate.4 = (bf16[16,768,256]{2,1,0:T(8,128)(2,1)}, bf16[64,512]{1,0:T(8,128)(2,1)S(1)}, bf16[64,512]{1,0:T(8,128)(2,1)S(1)}, bf16[64,512]{1,0:T(8,128)(2,1)S(1)}, bf16[64,512]{1,0:T(8,128)(2,1)S(1)}) custom-call(s32[19]{0:T(128)S(1)} %pad_add_fusion.meta, bf16[16,768,256]{2,1,0:T(8,128)(2,1)} %act.7, bf16[2,64,256]{2,1,0:T(8,128)(2,1)S(1)} %collective-permute-done.8.low, ...), custom_call_target="tpu_custom_call" | custom-call | flops 268435456 | bytes 1572864 | tf_op jit(solution)/shard_map/propagate/pallas_call | solution.py:126
  42.8 1.6 collective-permute-start.10
  44.4 9.4 %propagate.5 = (bf16[16,768,256]{2,1,0:T(8,128)(2,1)}, bf16[128,512]{1,0:T(8,128)(2,1)S(1)}, bf16[128,512]{1,0:T(8,128)(2,1)S(1)}, bf16[128,512]{1,0:T(8,128)(2,1)S(1)}, bf16[128,512]{1,0:T(8,128)(2,1)S(1)}) custom-call(s32[19]{0:T(128)S(1)} %pad_add_fusion.meta, bf16[16,768,256]{2,1,0:T(8,128)(2,1)} %act.7, ...), custom_call_target="tpu_custom_call", output_to_operand_aliasing={{0}: (9, {})} | custom-call | flops 536870912 | bytes 3145728 | tf_op jit(solution)/shard_map/propagate/pallas_call | solution.py:126
  53.8 1.6 collective-permute-start.11
  55.4 12.5 %propagate.6 = (bf16[16,768,256]{2,1,0:T(8,128)(2,1)}, bf16[192,512]{1,0:T(8,128)(2,1)S(1)}, bf16[192,512]{1,0:T(8,128)(2,1)S(1)}, bf16[192,512]{1,0:T(8,128)(2,1)}, bf16[192,512]{1,0:T(8,128)(2,1)}) custom-call(s32[19]{0:T(128)S(1)} %pad_add_fusion.meta, bf16[16,768,256]{2,1,0:T(8,128)(2,1)} %act.7, ...), custom_call_target="tpu_custom_call", output_to_operand_aliasing={{0}: (9, {})} | custom-call | flops 805306368 | bytes 4718592 | tf_op jit(solution)/shard_map/propagate/pallas_call | solution.py:126
  73.6 21.8 %propagate.7 = (bf16[16,768,256]{2,1,0:T(8,128)(2,1)}, bf16[384,512]{1,0:T(8,128)(2,1)S(1)}, bf16[384,512]{1,0:T(8,128)(2,1)}, bf16[384,512]{1,0:T(8,128)(2,1)}, bf16[384,512]{1,0:T(8,128)(2,1)}) custom-call(s32[19]{0:T(128)S(1)} %pad_add_fusion.meta, bf16[16,768,256]{2,1,0:T(8,128)(2,1)} %act.7, ...), custom_call_target="tpu_custom_call", output_to_operand_aliasing={{0}: (9, {})} | custom-call | flops 1610612736 | bytes 9437184 | tf_op jit(solution)/shard_map/propagate/pallas_call | solution.py:126
  96.1 1.6 collective-permute-start.17
  106.2 1.6 reshape.51.sel
  108.3 6.3 %collective-permute-done.19.rest_13_ = bf16[384,512]{1,0:T(8,128)(2,1)S(1)} collective-permute-done((bf16[384,512]{1,0:T(8,128)(2,1)}, bf16[384,512]{1,0:T(8,128)(2,1)S(1)}, u32[]{:S(2)}, u32[]{:S(2)}) %collective-permute-start.19) | collective-permute-done | bytes 393248 | tf_op jit(solution)/shard_map/ppermute | solution.py:344
  114.6 9.9 %collective-permute-done.20.rest_14_ = bf16[384,512]{1,0:T(8,128)(2,1)S(1)} collective-permute-done((bf16[384,512]{1,0:T(8,128)(2,1)}, bf16[384,512]{1,0:T(8,128)(2,1)S(1)}, u32[]{:S(2)}, u32[]{:S(2)}) %collective-permute-start.20) | collective-permute-done | bytes 393248 | tf_op jit(solution)/shard_map/ppermute | solution.py:344
  132.5 8.4 %couple.6 = (bf16[192,512]{1,0:T(8,128)(2,1)S(1)}, bf16[192,512]{1,0:T(8,128)(2,1)S(1)}, bf16[192,512]{1,0:T(8,128)(2,1)S(1)}, bf16[192,512]{1,0:T(8,128)(2,1)S(1)}) custom-call(s32[19]{0:T(128)S(1)} %pad_add_fusion.meta, f32[48,3072]{1,0:T(8,128)S(1)} %reshape.51.sel, bf16[2,64,6144]{2,1,0:T(8,128)(2,1)S(1)} %pad_maximum_fusion.tt, ...), custom_call_target="tpu_custom_call" | custom-call | flops 2415919104 | bytes 3932160 | tf_op jit(solution)/shard_map/couple/pallas_call | solution.py:188
  143.0 8.4 %couple.5 = (bf16[192,512]{1,0:T(8,128)(2,1)S(1)}, bf16[192,512]{1,0:T(8,128)(2,1)S(1)}, bf16[192,512]{1,0:T(8,128)(2,1)S(1)}, bf16[192,512]{1,0:T(8,128)(2,1)S(1)}) custom-call(s32[19]{0:T(128)S(1)} %pad_add_fusion.meta, f32[48,3072]{1,0:T(8,128)S(1)} %reshape.51.sel, bf16[2,64,6144]{2,1,0:T(8,128)(2,1)S(1)} %pad_maximum_fusion.tt, ...), custom_call_target="tpu_custom_call" | custom-call | flops 2415919104 | bytes 3932160 | tf_op jit(solution)/shard_map/couple/pallas_call | solution.py:188
  154.9 8.4 %couple.4 = (bf16[192,512]{1,0:T(8,128)(2,1)S(1)}, bf16[192,512]{1,0:T(8,128)(2,1)S(1)}, bf16[192,512]{1,0:T(8,128)(2,1)S(1)}, bf16[192,512]{1,0:T(8,128)(2,1)S(1)}) custom-call(s32[19]{0:T(128)S(1)} %pad_add_fusion.meta, f32[48,3072]{1,0:T(8,128)S(1)} %reshape.51.sel, bf16[2,64,6144]{2,1,0:T(8,128)(2,1)S(1)} %pad_maximum_fusion.tt, ...), custom_call_target="tpu_custom_call" | custom-call | flops 2415919104 | bytes 3932160 | tf_op jit(solution)/shard_map/couple/pallas_call | solution.py:188
  168.4 8.4 %couple.7 = (bf16[192,512]{1,0:T(8,128)(2,1)S(1)}, bf16[192,512]{1,0:T(8,128)(2,1)S(1)}, bf16[192,512]{1,0:T(8,128)(2,1)S(1)}, bf16[192,512]{1,0:T(8,128)(2,1)S(1)}) custom-call(s32[19]{0:T(128)S(1)} %pad_add_fusion.meta, f32[48,3072]{1,0:T(8,128)S(1)} %reshape.51.sel, bf16[2,64,6144]{2,1,0:T(8,128)(2,1)S(1)} %pad_maximum_fusion.tt, ...), custom_call_target="tpu_custom_call" | custom-call | flops 2415919104 | bytes 3932160 | tf_op jit(solution)/shard_map/couple/pallas_call | solution.py:188
  180.4 5.0 %finish.4.moved = bf16[16,768,256]{2,1,0:T(8,128)(2,1)} custom-call(s32[19]{0:T(128)S(1)} %pad_add_fusion.meta, s32[16,256]{1,0:T(8,128)S(1)} %fusion.1.slot, bf16[16,768,256]{2,1,0:T(8,128)(2,1)} %get-tuple-element.44.moved, bf16[192,512]{1,0:T(8,128)(2,1)S(1)} %get-tuple-element.61.rest_0_, ...), custom_call_target="tpu_custom_call", output_to_operand_aliasing={{}: (2, {})} | custom-call | flops 805306368 | bytes 3145728 | tf_op jit(solution)/shard_map/finish/pallas_call | solution.py:247
  185.4 5.0 %finish.5.moved = bf16[16,768,256]{2,1,0:T(8,128)(2,1)} custom-call(s32[19]{0:T(128)S(1)} %pad_add_fusion.meta, s32[16,256]{1,0:T(8,128)S(1)} %fusion.1.slot, bf16[16,768,256]{2,1,0:T(8,128)(2,1)} %finish.4.moved, bf16[192,512]{1,0:T(8,128)(2,1)S(1)} %get-tuple-element.65.rest_0_, ...), custom_call_target="tpu_custom_call", output_to_operand_aliasing={{}: (2, {})} | custom-call | flops 805306368 | bytes 3145728 | tf_op jit(solution)/shard_map/finish/pallas_call | solution.py:247
  190.5 5.0 %finish.6.moved = bf16[16,768,256]{2,1,0:T(8,128)(2,1)} custom-call(s32[19]{0:T(128)S(1)} %pad_add_fusion.meta, s32[16,256]{1,0:T(8,128)S(1)} %fusion.1.slot, bf16[16,768,256]{2,1,0:T(8,128)(2,1)} %finish.5.moved, bf16[192,512]{1,0:T(8,128)(2,1)S(1)} %get-tuple-element.69.rest_0_, ...), custom_call_target="tpu_custom_call", output_to_operand_aliasing={{}: (2, {})} | custom-call | flops 805306368 | bytes 3145728 | tf_op jit(solution)/shard_map/finish/pallas_call | solution.py:247
  195.5 5.0 %finish.7 = bf16[16,768,256]{2,1,0:T(8,128)(2,1)} custom-call(s32[19]{0:T(128)S(1)} %pad_add_fusion.meta, s32[16,256]{1,0:T(8,128)S(1)} %fusion.1.slot, bf16[16,768,256]{2,1,0:T(8,128)(2,1)} %finish.6.moved, bf16[192,512]{1,0:T(8,128)(2,1)S(1)} %get-tuple-element.73.rest_0_, ...), custom_call_target="tpu_custom_call", output_to_operand_aliasing={{}: (2, {})} | custom-call | flops 805306368 | bytes 3145728 | tf_op jit(solution)/shard_map/finish/pallas_call | solution.py:247
  (142 shorter events, 51.8 us)
Async XLA Ops:
  0.7 22.6 %collective-permute-start.2 = (f32[2,1,256]{2,1,0:T(1,128)S(1)}, f32[2,1,256]{2,1,0:T(1,128)S(1)}, u32[]{:S(2)}, u32[]{:S(2)}) collective-permute-start(f32[2,1,256]{2,1,0:T(1,128)S(1)} %get-tuple-element.89), channel_id=1, source_target_pairs={{0,1},{1,2},{2,3},{3,4},{4,5},{5,6},{6,7},{8,9},{9,10},{10,11},{11... | collective-permute-start | bytes 6152 | tf_op jit(solution)/shard_map/ppermute | solution.py:275
  3.1 21.6 %collective-permute-start.3 = (f32[2,1,256]{2,1,0:T(1,128)S(1)}, f32[2,1,256]{2,1,0:T(1,128)S(1)}, u32[]{:S(2)}, u32[]{:S(2)}) collective-permute-start(f32[2,1,256]{2,1,0:T(1,128)S(1)} %get-tuple-element.90), channel_id=1, source_target_pairs={{1,0},{2,1},{3,2},{4,3},{5,4},{6,5},{7,6},{9,8},{10,9},{11,10},{12... | collective-permute-start | bytes 6152 | tf_op jit(solution)/shard_map/ppermute | solution.py:276
  5.3 23.7 %collective-permute-start.8 = (bf16[2,64,256]{2,1,0:T(8,128)(2,1)S(1)}, bf16[2,64,256]{2,1,0:T(8,128)(2,1)S(1)}, u32[]{:S(2)}, u32[]{:S(2)}) collective-permute-start(bf16[2,64,256]{2,1,0:T(8,128)(2,1)S(1)} %get-tuple-element.80), channel_id=1, source_target_pairs={{0,1},{1,2},{2,3},{3,4},{4,5},{5,6},{6,7},{8,9},{9,10},{10,11},{11... | collective-permute-start | bytes 196616 | tf_op jit(solution)/shard_map/ppermute | solution.py:275
  10.5 19.8 %collective-permute-start.9 = (bf16[2,64,256]{2,1,0:T(8,128)(2,1)S(1)}, bf16[2,64,256]{2,1,0:T(8,128)(2,1)S(1)}, u32[]{:S(2)}, u32[]{:S(2)}) collective-permute-start(bf16[2,64,256]{2,1,0:T(8,128)(2,1)S(1)} %get-tuple-element.79), channel_id=1, source_target_pairs={{1,0},{2,1},{3,2},{4,3},{5,4},{6,5},{7,6},{9,8},{10,9},{11,10},{12... | collective-permute-start | bytes 196616 | tf_op jit(solution)/shard_map/ppermute | solution.py:276
  12.8 28.5 %collective-permute-start.6 = (bf16[2,128,256]{2,1,0:T(8,128)(2,1)S(1)}, bf16[2,128,256]{2,1,0:T(8,128)(2,1)S(1)}, u32[]{:S(2)}, u32[]{:S(2)}) collective-permute-start(bf16[2,128,256]{2,1,0:T(8,128)(2,1)S(1)} %get-tuple-element.82), channel_id=1, source_target_pairs={{0,1},{1,2},{2,3},{3,4},{4,5},{5,6},{6,7},{8,9},{9,10},{10,11},{11... | collective-permute-start | bytes 393224 | tf_op jit(solution)/shard_map/ppermute | solution.py:275
  23.4 19.4 %collective-permute-start.7 = (bf16[2,128,256]{2,1,0:T(8,128)(2,1)S(1)}, bf16[2,128,256]{2,1,0:T(8,128)(2,1)S(1)}, u32[]{:S(2)}, u32[]{:S(2)}) collective-permute-start(bf16[2,128,256]{2,1,0:T(8,128)(2,1)S(1)} %get-tuple-element.81), channel_id=1, source_target_pairs={{1,0},{2,1},{3,2},{4,3},{5,4},{6,5},{7,6},{9,8},{10,9},{11,10},{12... | collective-permute-start | bytes 393224 | tf_op jit(solution)/shard_map/ppermute | solution.py:276
  24.7 29.1 %collective-permute-start.4 = (bf16[2,192,256]{2,1,0:T(8,128)(2,1)S(1)}, bf16[2,192,256]{2,1,0:T(8,128)(2,1)S(1)}, u32[]{:S(2)}, u32[]{:S(2)}) collective-permute-start(bf16[2,192,256]{2,1,0:T(8,128)(2,1)S(1)} %get-tuple-element.84), channel_id=1, source_target_pairs={{0,1},{1,2},{2,3},{3,4},{4,5},{5,6},{6,7},{8,9},{9,10},{10,11},{11... | collective-permute-start | bytes 589832 | tf_op jit(solution)/shard_map/ppermute | solution.py:275
  29.0 26.4 %collective-permute-start.5 = (bf16[2,192,256]{2,1,0:T(8,128)(2,1)S(1)}, bf16[2,192,256]{2,1,0:T(8,128)(2,1)S(1)}, u32[]{:S(2)}, u32[]{:S(2)}) collective-permute-start(bf16[2,192,256]{2,1,0:T(8,128)(2,1)S(1)} %get-tuple-element.83), channel_id=1, source_target_pairs={{1,0},{2,1},{3,2},{4,3},{5,4},{6,5},{7,6},{9,8},{10,9},{11,10},{12... | collective-permute-start | bytes 589832 | tf_op jit(solution)/shard_map/ppermute | solution.py:276
  30.3 40.3 %collective-permute-start = (bf16[2,384,256]{2,1,0:T(8,128)(2,1)S(1)}, bf16[2,384,256]{2,1,0:T(8,128)(2,1)S(1)}, u32[]{:S(2)}, u32[]{:S(2)}) collective-permute-start(bf16[2,384,256]{2,1,0:T(8,128)(2,1)S(1)} %get-tuple-element.86), channel_id=1, source_target_pairs={{0,1},{1,2},{2,3},{3,4},{4,5},{5,6},{6,7},{8,9},{9,10},{10,11},{11... | collective-permute-start | bytes 1179656 | tf_op jit(solution)/shard_map/ppermute | solution.py:275
  41.3 30.8 %collective-permute-start.1 = (bf16[2,384,256]{2,1,0:T(8,128)(2,1)S(1)}, bf16[2,384,256]{2,1,0:T(8,128)(2,1)S(1)}, u32[]{:S(2)}, u32[]{:S(2)}) collective-permute-start(bf16[2,384,256]{2,1,0:T(8,128)(2,1)S(1)} %get-tuple-element.85), channel_id=1, source_target_pairs={{1,0},{2,1},{3,2},{4,3},{5,4},{6,5},{7,6},{9,8},{10,9},{11,10},{12... | collective-permute-start | bytes 1179656 | tf_op jit(solution)/shard_map/ppermute | solution.py:276
  42.8 25.8 %collective-permute-start.10 = (bf16[64,512]{1,0:T(8,128)(2,1)S(1)}, bf16[64,512]{1,0:T(8,128)(2,1)S(1)}, u32[]{:S(2)}, u32[]{:S(2)}) collective-permute-start(bf16[64,512]{1,0:T(8,128)(2,1)S(1)} %get-tuple-element.46), channel_id=1, source_target_pairs={{0,8},{8,0},{16,24},{24,16},{1,9},{9,1},{17,25},{25,17},{2,10},{10... | collective-permute-start | bytes 196616 | tf_op jit(solution)/shard_map/ppermute | solution.py:344
  68.0 35.1 %collective-permute-start.16 = (bf16[192,512]{1,0:T(8,128)(2,1)S(1)}, bf16[192,512]{1,0:T(8,128)(2,1)S(1)}, u32[]{:S(2)}, u32[]{:S(2)}) collective-permute-start(bf16[192,512]{1,0:T(8,128)(2,1)S(1)} %get-tuple-element.54), channel_id=1, source_target_pairs={{0,8},{8,0},{16,24},{24,16},{1,9},{9,1},{17,25},{25,17},{2,10},{10... | collective-permute-start | bytes 589832 | tf_op jit(solution)/shard_map/ppermute | solution.py:344
  68.6 26.8 %collective-permute-start.12 = (bf16[64,512]{1,0:T(8,128)(2,1)S(1)}, bf16[64,512]{1,0:T(8,128)(2,1)S(1)}, u32[]{:S(2)}, u32[]{:S(2)}) collective-permute-start(bf16[64,512]{1,0:T(8,128)(2,1)S(1)} %get-tuple-element.48), channel_id=1, source_target_pairs={{0,24},{8,16},{16,8},{24,0},{1,25},{9,17},{17,9},{25,1},{2,26},{10... | collective-permute-start | bytes 196616 | tf_op jit(solution)/shard_map/ppermute | solution.py:344
  70.1 27.5 %collective-permute-start.13 = (bf16[128,512]{1,0:T(8,128)(2,1)S(1)}, bf16[128,512]{1,0:T(8,128)(2,1)S(1)}, u32[]{:S(2)}, u32[]{:S(2)}) collective-permute-start(bf16[128,512]{1,0:T(8,128)(2,1)S(1)} %get-tuple-element.50), channel_id=1, source_target_pairs={{0,8},{8,0},{16,24},{24,16},{1,9},{9,1},{17,25},{25,17},{2,10},{10... | collective-permute-start | bytes 393224 | tf_op jit(solution)/shard_map/ppermute | solution.py:344
  70.6 28.1 %collective-permute-start.14 = (bf16[128,512]{1,0:T(8,128)(2,1)S(1)}, bf16[128,512]{1,0:T(8,128)(2,1)S(1)}, u32[]{:S(2)}, u32[]{:S(2)}) collective-permute-start(bf16[128,512]{1,0:T(8,128)(2,1)S(1)} %get-tuple-element.51), channel_id=1, source_target_pairs={{0,16},{8,24},{16,0},{24,8},{1,17},{9,25},{17,1},{25,9},{2,18},{10... | collective-permute-start | bytes 393224 | tf_op jit(solution)/shard_map/ppermute | solution.py:344
  72.2 28.7 %collective-permute-start.15 = (bf16[128,512]{1,0:T(8,128)(2,1)S(1)}, bf16[128,512]{1,0:T(8,128)(2,1)S(1)}, u32[]{:S(2)}, u32[]{:S(2)}) collective-permute-start(bf16[128,512]{1,0:T(8,128)(2,1)S(1)} %get-tuple-element.52), channel_id=1, source_target_pairs={{0,24},{8,16},{16,8},{24,0},{1,25},{9,17},{17,9},{25,1},{2,26},{10... | collective-permute-start | bytes 393224 | tf_op jit(solution)/shard_map/ppermute | solution.py:344
  101.6 23.0 %collective-permute-start.20 = (bf16[384,512]{1,0:T(8,128)(2,1)}, bf16[384,512]{1,0:T(8,128)(2,1)S(1)}, u32[]{:S(2)}, u32[]{:S(2)}) collective-permute-start(bf16[384,512]{1,0:T(8,128)(2,1)} %get-tuple-element.59), channel_id=1, source_target_pairs={{0,16},{8,24},{16,0},{24,8},{1,17},{9,25},{17,1},{25,9},{2,18},{10... | collective-permute-start | bytes 1179656 | tf_op jit(solution)/shard_map/ppermute | solution.py:344
  103.8 20.7 %collective-permute-start.21 = (bf16[384,512]{1,0:T(8,128)(2,1)}, bf16[384,512]{1,0:T(8,128)(2,1)}, u32[]{:S(2)}, u32[]{:S(2)}) collective-permute-start(bf16[384,512]{1,0:T(8,128)(2,1)} %get-tuple-element.60), channel_id=1, source_target_pairs={{0,24},{8,16},{16,8},{24,0},{1,25},{9,17},{17,9},{25,1},{2,26},{10... | collective-permute-start | bytes 1179656 | tf_op jit(solution)/shard_map/ppermute | solution.py:344
  140.9 22.5 %collective-permute-start.28 = (bf16[192,512]{1,0:T(8,128)(2,1)S(1)}, bf16[192,512]{1,0:T(8,128)(2,1)S(1)}, u32[]{:S(2)}, u32[]{:S(2)}) collective-permute-start(bf16[192,512]{1,0:T(8,128)(2,1)S(1)} %get-tuple-element.70), channel_id=1, source_target_pairs={{0,8},{8,0},{16,24},{24,16},{1,9},{9,1},{17,25},{25,17},{2,10},{10... | collective-permute-start | bytes 589832 | tf_op jit(solution)/shard_map/ppermute | solution.py:352
  141.5 49.0 %collective-permute-start.29 = (bf16[192,512]{1,0:T(8,128)(2,1)S(1)}, bf16[192,512]{1,0:T(8,128)(2,1)S(1)}, u32[]{:S(2)}, u32[]{:S(2)}) collective-permute-start(bf16[192,512]{1,0:T(8,128)(2,1)S(1)} %get-tuple-element.71), channel_id=1, source_target_pairs={{0,16},{8,24},{16,0},{24,8},{1,17},{9,25},{17,1},{25,9},{2,18},{10... | collective-permute-start | bytes 589832 | tf_op jit(solution)/shard_map/ppermute | solution.py:352
  163.4 27.1 %collective-permute-start.30 = (bf16[192,512]{1,0:T(8,128)(2,1)S(1)}, bf16[192,512]{1,0:T(8,128)(2,1)S(1)}, u32[]{:S(2)}, u32[]{:S(2)}) collective-permute-start(bf16[192,512]{1,0:T(8,128)(2,1)S(1)} %get-tuple-element.72), channel_id=1, source_target_pairs={{0,24},{8,16},{16,8},{24,0},{1,25},{9,17},{17,9},{25,1},{2,26},{10... | collective-permute-start | bytes 589832 | tf_op jit(solution)/shard_map/ppermute | solution.py:352
  176.8 18.7 %collective-permute-start.31 = (bf16[192,512]{1,0:T(8,128)(2,1)S(1)}, bf16[192,512]{1,0:T(8,128)(2,1)S(1)}, u32[]{:S(2)}, u32[]{:S(2)}) collective-permute-start(bf16[192,512]{1,0:T(8,128)(2,1)S(1)} %get-tuple-element.74), channel_id=1, source_target_pairs={{0,8},{8,0},{16,24},{24,16},{1,9},{9,1},{17,25},{25,17},{2,10},{10... | collective-permute-start | bytes 589832 | tf_op jit(solution)/shard_map/ppermute | solution.py:352
  177.4 18.1 %collective-permute-start.32 = (bf16[192,512]{1,0:T(8,128)(2,1)S(1)}, bf16[192,512]{1,0:T(8,128)(2,1)S(1)}, u32[]{:S(2)}, u32[]{:S(2)}) collective-permute-start(bf16[192,512]{1,0:T(8,128)(2,1)S(1)} %get-tuple-element.75), channel_id=1, source_target_pairs={{0,16},{8,24},{16,0},{24,8},{1,17},{9,25},{17,1},{25,9},{2,18},{10... | collective-permute-start | bytes 589832 | tf_op jit(solution)/shard_map/ppermute | solution.py:352
  178.9 16.6 %collective-permute-start.33 = (bf16[192,512]{1,0:T(8,128)(2,1)S(1)}, bf16[192,512]{1,0:T(8,128)(2,1)S(1)}, u32[]{:S(2)}, u32[]{:S(2)}) collective-permute-start(bf16[192,512]{1,0:T(8,128)(2,1)S(1)} %get-tuple-element.76), channel_id=1, source_target_pairs={{0,24},{8,16},{16,8},{24,0},{1,25},{9,17},{17,9},{25,1},{2,26},{10... | collective-permute-start | bytes 589832 | tf_op jit(solution)/shard_map/ppermute | solution.py:352
  (38 other events, 442.2 us)

commit v2 on v1

v2 whole, which is shorter than its diff:
```python
import functools

import jax
import jax.numpy as jnp
from jax import lax
from jax.experimental import pallas as pl
from jax.experimental.pallas import tpu as pltpu
from jax.sharding import PartitionSpec as P

NF = 64
ND = 48
SEA = 2048
WINDOW = 512
STEP = 256
SUBK = 16
courant_scale = 0.45
VMEM_LIMIT = 24 * 1024 * 1024


def split_directions(count, sizes):
    if sum(sizes) == count:
        return sizes
    return (1,) * count


def offsets_of(sizes):
    return [sum(sizes[:i]) for i in range(len(sizes))]


def setup_kernel(rows, bases, slot, slot_t, pattern, table, onehot, spread, sel, tt):
    lon = slot.shape[1]
    lanes = lax.broadcasted_iota(jnp.int32, (lon, WINDOW), 1)
    depths = lax.broadcasted_iota(jnp.int32, (WINDOW, lon), 0)
    for r in range(rows):
        base = bases[r]
        onehot[r] = jnp.where(slot_t[:, r:r + 1] - base == lanes, 1.0, 0.0).astype(jnp.bfloat16)
        spread[r] = jnp.where(slot[r:r + 1, :] - base == depths, 1.0, 0.0).astype(jnp.bfloat16)
    columns = [jnp.broadcast_to(pattern[:, j:j + 1], (ND, 128)) for j in range(pattern.shape[1])]
    which = lax.broadcasted_iota(jnp.int32, (ND, 128), 1) // NF
    for t in range(ND * NF // 128):
        target = which + t * (128 // NF)
        hit = columns[0] == target
        for column in columns[1:]:
            hit = hit | (column == target)
        sel[:, t * 128:(t + 1) * 128] = jnp.where(hit, 1.0, 0.0)
    for odd in range(2):
        for t in range(ND // 2):
            pair = jnp.concatenate(
                [table[2 * t + odd].astype(jnp.float32), table[(2 * t + odd + 1) % ND].astype(jnp.float32)],
                axis=1,
            ).astype(jnp.bfloat16)
            tt[odd, :, t * 128:(t + 1) * 128] = pair
            tt[odd, :, ND * NF + t * 128:ND * NF + (t + 1) * 128] = pair


def setup(bases, slot, slot_t, pattern, table):
    rows, lon = slot.shape
    vmem = pl.BlockSpec(memory_space=pltpu.VMEM)
    return pl.pallas_call(
        functools.partial(setup_kernel, rows),
        in_specs=[pl.BlockSpec(memory_space=pltpu.SMEM)] + [vmem] * 4,
        out_specs=[vmem] * 4,
        out_shape=[
            jax.ShapeDtypeStruct((rows, lon, WINDOW), jnp.bfloat16),
            jax.ShapeDtypeStruct((rows, WINDOW, lon), jnp.bfloat16),
            jax.ShapeDtypeStruct((ND, ND * NF), jnp.float32),
            jax.ShapeDtypeStruct((2, NF, 2 * ND * NF), jnp.bfloat16),
        ],
        compiler_params=pltpu.CompilerParams(vmem_limit_bytes=VMEM_LIMIT),
        cost_estimate=pl.CostEstimate(
            flops=8 * 2 ** 20, bytes_accessed=12 * 2 ** 20, transcendentals=0
        ),
        name="setup",
    )(bases, slot, slot_t, pattern, table)


def propagate_kernel(rows, peers, share, meta, act, low, high, ae_ref, an_ref, be_ref, bn_ref, onehot, *rest):
    moved = rest[-(peers + 2)]
    outs = rest[-(peers + 1):-1]
    packed = rest[-1]
    lon = act.shape[2]
    depth = act.shape[1]
    halves = lon // 128
    lane = lax.broadcasted_iota(jnp.int32, (SUBK, 128), 1)
    first = lane == 0
    last = lane == 127

    def group(i, carry):
        ks = pl.ds(pl.multiple_of(i * SUBK, SUBK), SUBK)
        ae = ae_ref[ks, :]
        an = an_ref[ks, :]

        def load(r):
            if r < 0:
                block = low[r + 2, ks, :]
            elif r < rows:
                block = act[r, ks, :]
            else:
                block = high[r - rows, ks, :]
            block = block.astype(jnp.float32)
            return [block[:, h * 128:(h + 1) * 128] for h in range(halves)]

        def parts(r):
            found = []
            for h in range(halves):
                ce = ae + be_ref[r + 1:r + 2, h * 128:(h + 1) * 128]
                cn = an + bn_ref[r + 1:r + 2, h * 128:(h + 1) * 128]
                found.append((ce > 0.0, jnp.abs(ce), cn > 0.0, jnp.abs(cn)))
            return found

        def advance(center, south, north, courant):
            right = [pltpu.roll(c, 1, 1) for c in center]
            left = [pltpu.roll(c, 127, 1) for c in center]
            result = []
            for h in range(halves):
                eastward, ce, northward, cn = courant[h]
                west = jnp.where(first, right[h - 1] if h else 0.0, right[h])
                east = jnp.where(last, left[h + 1] if h < halves - 1 else 0.0, left[h])
                along = jnp.where(eastward, west, east)
                across = jnp.where(northward, south[h], north[h])
                c = center[h]
                result.append(c - ce * (c - along) - cn * (c - across))
            return result

        below, here = load(-2), load(-1)
        once = {}
        courant = {}
        for r in range(-1, rows + 1):
            above = load(r + 1)
            courant[r] = parts(r)
            value = advance(here, below, above, courant[r])
            if r == -1:
                value = [jnp.where(meta[1] > 0, v, 0.0) for v in value]
            if r == rows:
                value = [jnp.where(meta[2] > 0, v, 0.0) for v in value]
            once[r] = value
            if r >= 1:
                twice = advance(once[r - 1], once[r - 2], once[r], courant[r - 1])
                for h in range(halves):
                    moved[r - 1, ks, h * 128:(h + 1) * 128] = twice[h].astype(jnp.bfloat16)
            below, here = here, above
        return carry

    lax.fori_loop(0, depth // SUBK, group, 0)

    packed[...] = jnp.zeros_like(packed)
    for r in range(rows):
        window = pl.ds(pl.multiple_of(meta[3 + r], STEP), WINDOW)
        part = jnp.dot(moved[r], onehot[r], preferred_element_type=jnp.float32)
        packed[:, window] += part.astype(jnp.bfloat16)
    me = meta[0]
    for k in range(peers):
        start = pl.multiple_of((me ^ k) * share, 128)
        outs[k][...] = packed[:, pl.ds(start, share)]


def propagate(meta, action, low, high, ae, an, be, bn, onehot, moved, begin, count, peers):
    rows, comps, lon = action.shape
    share = SEA // peers
    which = begin // count
    depth = count * NF
    here = lambda s, m: (0, which, 0)
    vmem = pl.BlockSpec(memory_space=pltpu.VMEM)
    in_specs = [
        pl.BlockSpec((rows, depth, lon), here),
        pl.BlockSpec((2, depth, lon), here),
        pl.BlockSpec((2, depth, lon), here),
        pl.BlockSpec((depth, 128), lambda s, m: (which, 0)),
        pl.BlockSpec((depth, 128), lambda s, m: (which, 0)),
        vmem,
        vmem,
        vmem,
    ]
    args = [meta, action, low, high, ae, an, be, bn, onehot]
    aliases = {}
    if moved is not None:
        in_specs.append(pl.BlockSpec(memory_space=pl.ANY))
        aliases = {len(args): 0}
        args.append(moved)
    cells = depth * rows * lon
    return pl.pallas_call(
        functools.partial(propagate_kernel, rows, peers, share),
        grid_spec=pltpu.PrefetchScalarGridSpec(
            num_scalar_prefetch=1,
            grid=(1,),
            in_specs=in_specs,
            out_specs=[pl.BlockSpec((rows, depth, lon), here)] + [vmem] * peers,
            scratch_shapes=[pltpu.VMEM((depth, SEA), jnp.bfloat16)],
        ),
        out_shape=[jax.ShapeDtypeStruct(action.shape, jnp.bfloat16)]
        + [jax.ShapeDtypeStruct((depth, share), jnp.bfloat16)] * peers,
        input_output_aliases=aliases,
        compiler_params=pltpu.CompilerParams(vmem_limit_bytes=VMEM_LIMIT),
        cost_estimate=pl.CostEstimate(
            flops=cells * 2 * WINDOW, bytes_accessed=cells * 6, transcendentals=0
        ),
        name="propagate",
    )(*args)


def couple_kernel(peers, dirs, begin, size, spots, meta, sel, tt, *rest):
    pieces = rest[:len(spots)]
    outs = rest[len(spots):len(spots) + peers]
    x, w, y, in_sem, out_sem = rest[len(spots) + peers:]
    me = meta[0]
    copies = []
    for i, (k, first) in enumerate(spots):
        depth = pieces[i].shape[0]
        start = pl.multiple_of(((me ^ k) * dirs + first) * NF, NF)
        copies.append(pltpu.make_async_copy(pieces[i], x.at[pl.ds(start, depth), :], in_sem.at[i]))
        copies[-1].start()

    def strip(i, carry):
        r = i // size * dirs + begin + i % size
        turn = lax.rem(ND - r, ND)
        lanes = pl.ds(pl.multiple_of((turn // 2) * 128, 128), ND * NF)
        keep = jnp.broadcast_to(sel[pl.ds(r, 1), :], (16, ND * NF)).astype(jnp.bfloat16)
        for q in range(NF // 16):
            w[pl.ds(pl.multiple_of(i * NF + q * 16, 16), 16), :] = tt[turn % 2, pl.ds(q * 16, 16), lanes] * keep
        return carry

    lax.fori_loop(0, peers * size, strip, 0)
    for copy in copies:
        copy.wait()
    coupled = jnp.dot(w[...], x[...], preferred_element_type=jnp.float32)
    for p in range(peers):
        own = x[(p * dirs + begin) * NF:(p * dirs + begin + size) * NF, :].astype(jnp.float32)
        y[p] = (own + own * coupled[p * size * NF:(p + 1) * size * NF]).astype(jnp.bfloat16)
    copies = []
    for k in range(peers):
        copies.append(pltpu.make_async_copy(y.at[me ^ k], outs[k], out_sem.at[k]))
        copies[-1].start()
    for copy in copies:
        copy.wait()


def couple(meta, sel, tt, pieces, spots, begin, size, peers, dirs):
    share = SEA // peers
    return pl.pallas_call(
        functools.partial(couple_kernel, peers, dirs, begin, size, spots),
        in_specs=[
            pl.BlockSpec(memory_space=pltpu.SMEM),
            pl.BlockSpec(memory_space=pltpu.VMEM),
            pl.BlockSpec(memory_space=pltpu.VMEM),
        ]
        + [pl.BlockSpec(memory_space=pl.ANY)] * len(pieces),
        out_specs=[pl.BlockSpec(memory_space=pl.ANY)] * peers,
        out_shape=[jax.ShapeDtypeStruct((size * NF, share), jnp.bfloat16)] * peers,
        scratch_shapes=[
            pltpu.VMEM((ND * NF, share), jnp.bfloat16),
            pltpu.VMEM((peers * size * NF, ND * NF), jnp.bfloat16),
            pltpu.VMEM((peers, size * NF, share), jnp.bfloat16),
            pltpu.SemaphoreType.DMA((len(pieces),)),
            pltpu.SemaphoreType.DMA((peers,)),
        ],
        compiler_params=pltpu.CompilerParams(vmem_limit_bytes=VMEM_LIMIT),
        cost_estimate=pl.CostEstimate(
            flops=2 * peers * size * NF * ND * NF * share,
            bytes_accessed=2 * (ND * NF + peers * size * NF) * share,
            transcendentals=0,
        ),
        name="couple",
    )(meta, sel, tt, *pieces)


def finish_kernel(peers, share, group, meta, slot, spread, moved, *rest):
    pieces = rest[:peers]
    out, renewed, sem = rest[peers:]
    me = meta[0]

    @pl.when(pl.program_id(0) == 0)
    def fetch():
        copies = []
        for k in range(peers):
            start = pl.multiple_of((me ^ k) * share, 128)
            copies.append(pltpu.make_async_copy(pieces[k], renewed.at[:, pl.ds(start, share)], sem.at[k]))
            copies[-1].start()
        for copy in copies:
            copy.wait()

    for i in range(group):
        r = pl.program_id(0) * group + i
        base = pl.multiple_of(meta[3 + r], STEP)
        cells = slot[pl.ds(r, 1), :]
        new = jnp.dot(renewed[:, pl.ds(base, WINDOW)], spread[r], preferred_element_type=jnp.float32)
        out[i] = jnp.where(cells >= 0, new, moved[i].astype(jnp.float32)).astype(jnp.bfloat16)


def finish(meta, slot, spread, moved, pieces, which, size, peers):
    rows, comps, lon = moved.shape
    share = SEA // peers
    group = 4
    block = pl.BlockSpec((group, size * NF, lon), lambda s, m: (s, which, 0))
    return pl.pallas_call(
        functools.partial(finish_kernel, peers, share, group),
        grid_spec=pltpu.PrefetchScalarGridSpec(
            num_scalar_prefetch=1,
            grid=(rows // group,),
            in_specs=[pl.BlockSpec(memory_space=pltpu.VMEM)] * 2 + [block]
            + [pl.BlockSpec(memory_space=pl.ANY)] * peers,
            out_specs=block,
            scratch_shapes=[
                pltpu.VMEM((size * NF, SEA), jnp.bfloat16),
                pltpu.SemaphoreType.DMA((peers,)),
            ],
        ),
        out_shape=jax.ShapeDtypeStruct(moved.shape, jnp.bfloat16),
        input_output_aliases={3: 0},
        compiler_params=pltpu.CompilerParams(vmem_limit_bytes=VMEM_LIMIT),
        cost_estimate=pl.CostEstimate(
            flops=2 * rows * size * NF * lon * WINDOW,
            bytes_accessed=4 * rows * size * NF * lon,
            transcendentals=0,
        ),
        name="finish",
    )(meta, slot, spread, moved, *pieces)


def pass_on(array, axis, up):
    count = lax.axis_size(axis)
    if up:
        return lax.ppermute(array, axis, [(i, i + 1) for i in range(count - 1)])
    return lax.ppermute(array, axis, [(i + 1, i) for i in range(count - 1)])


def local(action, east_current, north_current, sea_mask, pattern, table):
    rows, comps, lon = action.shape
    peers = lax.axis_size("spec")
    me = lax.axis_index("spec")
    tile = lax.axis_index("tile")
    tiles = lax.axis_size("tile")
    dirs = comps // NF
    parts_out = split_directions(dirs, (3, 3, 3, 3))
    parts_back = split_directions(dirs, (3, 3, 3, 3))

    def edge(row):
        pair = jnp.concatenate([east_current[row:row + 1], north_current[row:row + 1]])
        coarse = lax.reduce_precision(pair, 8, 7)
        fine = pair - coarse
        tail = jnp.concatenate([coarse, fine, jnp.zeros((12, lon), jnp.float32)])
        return jnp.broadcast_to(tail.astype(jnp.bfloat16), (2, 16, lon))

    low = pass_on(jnp.concatenate([action[rows - 2:], edge(rows - 1)], axis=1), "tile", True)
    high = pass_on(jnp.concatenate([action[:2], edge(0)], axis=1), "tile", False)
    low_current = low[0, comps:comps + 4].astype(jnp.float32)
    high_current = high[0, comps:comps + 4].astype(jnp.float32)
    be, bn = [
        courant_scale
        * jnp.concatenate([
            low_current[i:i + 1] + low_current[i + 2:i + 3],
            own,
            high_current[i:i + 1] + high_current[i + 2:i + 3],
        ])
        for i, own in enumerate((east_current, north_current))
    ]

    components = me * comps + jnp.arange(comps, dtype=jnp.int32)
    direction = (components // NF).astype(jnp.float32)
    frequency = (components % NF).astype(jnp.float32)
    speed = courant_scale * jnp.exp(-2.0 * frequency / (NF - 1))
    theta = 2.0 * jnp.pi * direction / ND
    ae = jnp.broadcast_to((speed * jnp.cos(theta))[:, None], (comps, 128))
    an = jnp.broadcast_to((speed * jnp.sin(theta))[:, None], (comps, 128))

    sea = sea_mask > 0
    before = jnp.dot(
        sea.astype(jnp.bfloat16),
        jnp.triu(jnp.ones((lon, lon), jnp.bfloat16), 1),
        preferred_element_type=jnp.float32,
    )
    totals = jnp.sum(sea.astype(jnp.float32), axis=1)
    starts = jnp.sum(
        jnp.where(jnp.tril(jnp.ones((rows, rows), jnp.bool_), -1), totals[None, :], 0.0), axis=1
    )
    slot = jnp.where(sea, (before + starts[:, None]).astype(jnp.int32), -1)
    bases = jnp.minimum(starts.astype(jnp.int32) // STEP * STEP, SEA - WINDOW)
    meta = jnp.concatenate([
        jnp.stack([me, (tile > 0).astype(jnp.int32), (tile < tiles - 1).astype(jnp.int32)]),
        bases,
    ]).astype(jnp.int32)
    slot_t = slot.T

    onehot, spread, sel, tt = setup(bases, slot, slot_t, pattern, table)

    moved = None
    pieces, spots = [], []
    for begin, count in zip(offsets_of(parts_out), parts_out):
        moved, *packed = propagate(
            meta, action, low, high, ae, an, be, bn, onehot, moved, begin, count, peers
        )
        for k in range(peers):
            piece = packed[k]
            if k:
                piece = lax.ppermute(piece, "spec", [(i, i ^ k) for i in range(peers)])
            pieces.append(piece)
            spots.append((k, begin))

    result = moved
    for g, (begin, size) in enumerate(zip(offsets_of(parts_back), parts_back)):
        renewed = couple(meta, sel, tt, pieces, tuple(spots), begin, size, peers, dirs)
        back = [renewed[0]] + [
            lax.ppermute(renewed[k], "spec", [(i, i ^ k) for i in range(peers)])
            for k in range(1, peers)
        ]
        result = finish(meta, slot, spread, result, back, begin // size, size, peers)
    return result


def solution(mesh):
    return jax.shard_map(
        local,
        mesh=mesh,
        in_specs=(
            P("tile", "spec", None),
            P("tile", None),
            P("tile", None),
            P("tile", None),
            P(),
            P(),
        ),
        out_specs=P("tile", "spec", None),
        check_vma=False,
    )
```

time: 202 us -> 165 us (0.82)
  the two profiles are of different devices: /device:TPU:0 before, /device:TPU:8 now
where the time goes in v2:
time: 165 us
  Pallas kernels  102 us (62%)
  starting transfers between devices  33.7 us (20%)
  waiting for transfers between devices  20.2 us (12%)
  local copies, waits for them, and re-layouts  6.4 us (4%)
    pallas_call x4, Pallas kernels, couple(): pl.pallas_call(functools.partial(couple_kernel, peers, dirs, begin, size,...  39.1 us
    pallas_call x4, Pallas kernels, propagate(): pl.pallas_call(functools.partial(propagate_kernel, rows, peers, share), g...  36.8 us
    pallas_call x4, Pallas kernels, finish(): pl.pallas_call(functools.partial(finish_kernel, peers, share, group), gri...  19.9 us
    ppermute x12, waiting for transfers between devices, local(): piece = lax.ppermute(piece, 'spec', [(i, i ^ k) for i in range(peers)])  17.5 us
    ppermute x12, starting transfers between devices, local(): lax.ppermute(renewed[k], 'spec', [(i, i ^ k) for i in range(peers)])  14.2 us
    ppermute x12, starting transfers between devices, local(): piece = lax.ppermute(piece, 'spec', [(i, i ^ k) for i in range(peers)])  14 us
    pallas_call x1, Pallas kernels, setup(): pl.pallas_call(functools.partial(setup_kernel, rows), in_specs=[pl.BlockS...  6.42 us
    ppermute x1, starting transfers between devices, pass_on(): return lax.ppermute(array, axis, [(i + 1, i) for i in range(count - 1)])  3.63 us
  transfers between devices with their start and end apart: 26, of which 7 were waited for; matrix products, arithmetic and copies ran while one was open for 1% of the time, Pallas kernels for 47%

profile of v2, /device:TPU:8, one launch (start us, length us, event | category | flops | bytes accessed | tf_op | source)
XLA Modules:
  0.0 164.8 jit_solution(14678427156883391217)
XLA Ops:
  6.1 3.6 %collective-permute-start.1 = (bf16[2,784,256]{2,1,0:T(8,128)(2,1)}, bf16[2,784,256]{2,1,0:T(8,128)(2,1)S(1)}, u32[]{:S(2)}, u32[]{:S(2)}) collective-permute-start(bf16[2,784,256]{2,1,0:T(8,128)(2,1)} %pad_maximum_fusion.1), channel_id=1, source_target_pairs={{1,0},{2,1},{3,2},{4,3},{5,4},{6,5},{7,6},{9,8},{10,9},{11,10},{12... | collective-permute-start | bytes 2408456 | tf_op jit(solution)/shard_map/ppermute | solution.py:323
  10.5 6.4 %setup.1 = (bf16[16,256,512]{2,1,0:T(8,128)(2,1)S(1)}, bf16[16,512,256]{2,1,0:T(8,128)(2,1)S(1)}, f32[48,3072]{1,0:T(8,128)S(1)}, bf16[2,64,6144]{2,1,0:T(8,128)(2,1)S(1)}) custom-call(s32[16]{0:T(128)S(1)} %multiply_minimum_fusion.bases, s32[16,256]{1,0:T(8,128)S(1)} %fusion.1.slot, s32[256,16]{1,0:T(8,128)S(1)} %copy.16.slot_t, ...), custom_call_target="tpu_custom_call" | custom-call | flops 8388608 | bytes 12582912 | tf_op jit(solution)/shard_map/setup/pallas_call | solution.py:59
  17.1 2.7 %collective-permute-done.1.high = bf16[2,784,256]{2,1,0:T(8,128)(2,1)S(1)} collective-permute-done((bf16[2,784,256]{2,1,0:T(8,128)(2,1)}, bf16[2,784,256]{2,1,0:T(8,128)(2,1)S(1)}, u32[]{:S(2)}, u32[]{:S(2)}) %collective-permute-start.1) | collective-permute-done | bytes 802848 | tf_op jit(solution)/shard_map/ppermute | solution.py:323
  20.2 2.8 %copy-done = bf16[16,768,256]{2,1,0:T(8,128)(2,1)S(1)} copy-done((bf16[16,768,256]{2,1,0:T(8,128)(2,1)S(1)}, bf16[16,768,256]{2,1,0:T(8,128)(2,1)}, u32[]{:S(2)}) %copy-start) | copy-done | bytes 6291480
  22.9 9.3 %propagate.4 = (bf16[16,768,256]{2,1,0:T(8,128)(2,1)}, bf16[192,512]{1,0:T(8,128)(2,1)S(1)}, bf16[192,512]{1,0:T(8,128)(2,1)S(1)}, bf16[192,512]{1,0:T(8,128)(2,1)S(1)}, bf16[192,512]{1,0:T(8,128)(2,1)S(1)}) custom-call(s32[19]{0:T(128)S(1)} %pad_add_fusion.meta, bf16[16,768,256]{2,1,0:T(8,128)(2,1)S(1)} %copy-done, ...), custom_call_target="tpu_custom_call" | custom-call | flops 805306368 | bytes 4718592 | tf_op jit(solution)/shard_map/propagate/pallas_call | solution.py:181
  35.8 9.2 %propagate.5 = (bf16[16,768,256]{2,1,0:T(8,128)(2,1)}, bf16[192,512]{1,0:T(8,128)(2,1)S(1)}, bf16[192,512]{1,0:T(8,128)(2,1)S(1)}, bf16[192,512]{1,0:T(8,128)(2,1)S(1)}, bf16[192,512]{1,0:T(8,128)(2,1)S(1)}) custom-call(s32[19]{0:T(128)S(1)} %pad_add_fusion.meta, bf16[16,768,256]{2,1,0:T(8,128)(2,1)S(1)} %copy-done, ...), custom_call_target="tpu_custom_call", output_to_operand_aliasing={{0}: (9, {})} | custom-call | flops 805306368 | bytes 4718592 | tf_op jit(solution)/shard_map/propagate/pallas_call | solution.py:181
  47.9 9.2 %propagate.6 = (bf16[16,768,256]{2,1,0:T(8,128)(2,1)}, bf16[192,512]{1,0:T(8,128)(2,1)S(1)}, bf16[192,512]{1,0:T(8,128)(2,1)S(1)}, bf16[192,512]{1,0:T(8,128)(2,1)S(1)}, bf16[192,512]{1,0:T(8,128)(2,1)S(1)}) custom-call(s32[19]{0:T(128)S(1)} %pad_add_fusion.meta, bf16[16,768,256]{2,1,0:T(8,128)(2,1)S(1)} %copy-done, ...), custom_call_target="tpu_custom_call", output_to_operand_aliasing={{0}: (9, {})} | custom-call | flops 805306368 | bytes 4718592 | tf_op jit(solution)/shard_map/propagate/pallas_call | solution.py:181
  57.1 9.2 %propagate.7 = (bf16[16,768,256]{2,1,0:T(8,128)(2,1)}, bf16[192,512]{1,0:T(8,128)(2,1)S(1)}, bf16[192,512]{1,0:T(8,128)(2,1)S(1)}, bf16[192,512]{1,0:T(8,128)(2,1)S(1)}, bf16[192,512]{1,0:T(8,128)(2,1)S(1)}) custom-call(s32[19]{0:T(128)S(1)} %pad_add_fusion.meta, bf16[16,768,256]{2,1,0:T(8,128)(2,1)S(1)} %copy-done, ...), custom_call_target="tpu_custom_call", output_to_operand_aliasing={{0}: (9, {})} | custom-call | flops 805306368 | bytes 4718592 | tf_op jit(solution)/shard_map/propagate/pallas_call | solution.py:181
  71.7 3.2 %collective-permute-done.7.rest_7_ = bf16[192,512]{1,0:T(8,128)(2,1)S(1)} collective-permute-done((bf16[192,512]{1,0:T(8,128)(2,1)S(1)}, bf16[192,512]{1,0:T(8,128)(2,1)S(1)}, u32[]{:S(2)}, u32[]{:S(2)}) %collective-permute-start.7) | collective-permute-done | bytes 196640 | tf_op jit(solution)/shard_map/ppermute | solution.py:394
  75.4 2.7 %collective-permute-done.11.rest_13_ = bf16[192,512]{1,0:T(8,128)(2,1)S(1)} collective-permute-done((bf16[192,512]{1,0:T(8,128)(2,1)S(1)}, bf16[192,512]{1,0:T(8,128)(2,1)S(1)}, u32[]{:S(2)}, u32[]{:S(2)}) %collective-permute-start.11) | collective-permute-done | bytes 196640 | tf_op jit(solution)/shard_map/ppermute | solution.py:394
  79.7 3.7 %collective-permute-done.13.rest_15_ = bf16[192,512]{1,0:T(8,128)(2,1)S(1)} collective-permute-done((bf16[192,512]{1,0:T(8,128)(2,1)S(1)}, bf16[192,512]{1,0:T(8,128)(2,1)S(1)}, u32[]{:S(2)}, u32[]{:S(2)}) %collective-permute-start.13) | collective-permute-done | bytes 196640 | tf_op jit(solution)/shard_map/ppermute | solution.py:394
  83.4 3.3 %collective-permute-done.8.rest_9_ = bf16[192,512]{1,0:T(8,128)(2,1)S(1)} collective-permute-done((bf16[192,512]{1,0:T(8,128)(2,1)S(1)}, bf16[192,512]{1,0:T(8,128)(2,1)S(1)}, u32[]{:S(2)}, u32[]{:S(2)}) %collective-permute-start.8) | collective-permute-done | bytes 196640 | tf_op jit(solution)/shard_map/ppermute | solution.py:394
  87.5 3.8 %collective-permute-done.10.rest_11_ = bf16[192,512]{1,0:T(8,128)(2,1)S(1)} collective-permute-done((bf16[192,512]{1,0:T(8,128)(2,1)S(1)}, bf16[192,512]{1,0:T(8,128)(2,1)S(1)}, u32[]{:S(2)}, u32[]{:S(2)}) %collective-permute-start.10) | collective-permute-done | bytes 196640 | tf_op jit(solution)/shard_map/ppermute | solution.py:394
  91.2 9.7 %couple.6 = (bf16[192,512]{1,0:T(8,128)(2,1)S(1)}, bf16[192,512]{1,0:T(8,128)(2,1)S(1)}, bf16[192,512]{1,0:T(8,128)(2,1)S(1)}, bf16[192,512]{1,0:T(8,128)(2,1)S(1)}) custom-call(s32[19]{0:T(128)S(1)} %pad_add_fusion.meta, f32[48,3072]{1,0:T(8,128)S(1)} %get-tuple-element.51.sel, bf16[2,64,6144]{2,1,0:T(8,128)(2,1)S(1)} %get-tuple-element.52.tt, ...), custom_call_target="tpu_custom_call" | custom-call | flops 2415919104 | bytes 3932160 | tf_op jit(solution)/shard_map/couple/pallas_call | solution.py:239
  102.1 9.7 %couple.5 = (bf16[192,512]{1,0:T(8,128)(2,1)S(1)}, bf16[192,512]{1,0:T(8,128)(2,1)S(1)}, bf16[192,512]{1,0:T(8,128)(2,1)S(1)}, bf16[192,512]{1,0:T(8,128)(2,1)S(1)}) custom-call(s32[19]{0:T(128)S(1)} %pad_add_fusion.meta, f32[48,3072]{1,0:T(8,128)S(1)} %get-tuple-element.51.sel, bf16[2,64,6144]{2,1,0:T(8,128)(2,1)S(1)} %get-tuple-element.52.tt, ...), custom_call_target="tpu_custom_call" | custom-call | flops 2415919104 | bytes 3932160 | tf_op jit(solution)/shard_map/couple/pallas_call | solution.py:239
  115.4 9.9 %couple.4 = (bf16[192,512]{1,0:T(8,128)(2,1)S(1)}, bf16[192,512]{1,0:T(8,128)(2,1)S(1)}, bf16[192,512]{1,0:T(8,128)(2,1)S(1)}, bf16[192,512]{1,0:T(8,128)(2,1)S(1)}) custom-call(s32[19]{0:T(128)S(1)} %pad_add_fusion.meta, f32[48,3072]{1,0:T(8,128)S(1)} %get-tuple-element.51.sel, bf16[2,64,6144]{2,1,0:T(8,128)(2,1)S(1)} %get-tuple-element.52.tt, ...), custom_call_target="tpu_custom_call" | custom-call | flops 2415919104 | bytes 3932160 | tf_op jit(solution)/shard_map/couple/pallas_call | solution.py:239
  125.3 2.5 %collective-permute-start.22 = (bf16[192,512]{1,0:T(8,128)(2,1)S(1)}, bf16[192,512]{1,0:T(8,128)(2,1)S(1)}, u32[]{:S(2)}, u32[]{:S(2)}) collective-permute-start(bf16[192,512]{1,0:T(8,128)(2,1)S(1)} %get-tuple-element.80), channel_id=1, source_target_pairs={{0,24},{8,16},{16,8},{24,0},{1,25},{9,17},{17,9},{25,1},{2,26},{10... | collective-permute-start | bytes 589832 | tf_op jit(solution)/shard_map/ppermute | solution.py:402
  128.9 2.4 %collective-permute-start.16 = (bf16[192,512]{1,0:T(8,128)(2,1)S(1)}, bf16[192,512]{1,0:T(8,128)(2,1)S(1)}, u32[]{:S(2)}, u32[]{:S(2)}) collective-permute-start(bf16[192,512]{1,0:T(8,128)(2,1)S(1)} %get-tuple-element.72), channel_id=1, source_target_pairs={{0,24},{8,16},{16,8},{24,0},{1,25},{9,17},{17,9},{25,1},{2,26},{10... | collective-permute-start | bytes 589832 | tf_op jit(solution)/shard_map/ppermute | solution.py:402
  131.3 9.7 %couple.7 = (bf16[192,512]{1,0:T(8,128)(2,1)S(1)}, bf16[192,512]{1,0:T(8,128)(2,1)S(1)}, bf16[192,512]{1,0:T(8,128)(2,1)S(1)}, bf16[192,512]{1,0:T(8,128)(2,1)S(1)}) custom-call(s32[19]{0:T(128)S(1)} %pad_add_fusion.meta, f32[48,3072]{1,0:T(8,128)S(1)} %get-tuple-element.51.sel, bf16[2,64,6144]{2,1,0:T(8,128)(2,1)S(1)} %get-tuple-element.52.tt, ...), custom_call_target="tpu_custom_call" | custom-call | flops 2415919104 | bytes 3932160 | tf_op jit(solution)/shard_map/couple/pallas_call | solution.py:239
  142.2 2.4 %collective-permute-start.25 = (bf16[192,512]{1,0:T(8,128)(2,1)S(1)}, bf16[192,512]{1,0:T(8,128)(2,1)S(1)}, u32[]{:S(2)}, u32[]{:S(2)}) collective-permute-start(bf16[192,512]{1,0:T(8,128)(2,1)S(1)} %get-tuple-element.84), channel_id=1, source_target_pairs={{0,24},{8,16},{16,8},{24,0},{1,25},{9,17},{17,9},{25,1},{2,26},{10... | collective-permute-start | bytes 589832 | tf_op jit(solution)/shard_map/ppermute | solution.py:402
  144.6 5.0 %finish.4.moved = bf16[16,768,256]{2,1,0:T(8,128)(2,1)} custom-call(s32[19]{0:T(128)S(1)} %pad_add_fusion.meta, s32[16,256]{1,0:T(8,128)S(1)} %fusion.1.slot, bf16[16,512,256]{2,1,0:T(8,128)(2,1)S(1)} %get-tuple-element.45.spread, bf16[16,768,256]{2,1,0:T(8,128)(2,1)} %get-tuple-element.50.moved, ...), custom_call_target="tpu_custom_call", output_to_operand_aliasing={{}: (3, {})} | custom-call | flops 805306368 | bytes 3145728 | tf_op jit(solution)/shard_map/finish/pallas_call | solution.py:294
  149.6 5.0 %finish.5.moved = bf16[16,768,256]{2,1,0:T(8,128)(2,1)} custom-call(s32[19]{0:T(128)S(1)} %pad_add_fusion.meta, s32[16,256]{1,0:T(8,128)S(1)} %fusion.1.slot, bf16[16,512,256]{2,1,0:T(8,128)(2,1)S(1)} %get-tuple-element.45.spread, bf16[16,768,256]{2,1,0:T(8,128)(2,1)} %finish.4.moved, ...), custom_call_target="tpu_custom_call", output_to_operand_aliasing={{}: (3, {})} | custom-call | flops 805306368 | bytes 3145728 | tf_op jit(solution)/shard_map/finish/pallas_call | solution.py:294
  154.6 5.0 %finish.6.moved = bf16[16,768,256]{2,1,0:T(8,128)(2,1)} custom-call(s32[19]{0:T(128)S(1)} %pad_add_fusion.meta, s32[16,256]{1,0:T(8,128)S(1)} %fusion.1.slot, bf16[16,512,256]{2,1,0:T(8,128)(2,1)S(1)} %get-tuple-element.45.spread, bf16[16,768,256]{2,1,0:T(8,128)(2,1)} %finish.5.moved, ...), custom_call_target="tpu_custom_call", output_to_operand_aliasing={{}: (3, {})} | custom-call | flops 805306368 | bytes 3145728 | tf_op jit(solution)/shard_map/finish/pallas_call | solution.py:294
  159.6 5.0 %finish.7 = bf16[16,768,256]{2,1,0:T(8,128)(2,1)} custom-call(s32[19]{0:T(128)S(1)} %pad_add_fusion.meta, s32[16,256]{1,0:T(8,128)S(1)} %fusion.1.slot, bf16[16,512,256]{2,1,0:T(8,128)(2,1)S(1)} %get-tuple-element.45.spread, bf16[16,768,256]{2,1,0:T(8,128)(2,1)} %finish.6.moved, ...), custom_call_target="tpu_custom_call", output_to_operand_aliasing={{}: (3, {})} | custom-call | flops 805306368 | bytes 3145728 | tf_op jit(solution)/shard_map/finish/pallas_call | solution.py:294
  (81 shorter events, 28.8 us)
Async XLA Ops:
  3.3 13.8 %collective-permute-start = (bf16[2,784,256]{2,1,0:T(8,128)(2,1)S(1)}, bf16[2,784,256]{2,1,0:T(8,128)(2,1)S(1)}, u32[]{:S(2)}, u32[]{:S(2)}) collective-permute-start(bf16[2,784,256]{2,1,0:T(8,128)(2,1)S(1)} %pad_maximum_fusion), channel_id=1, source_target_pairs={{0,1},{1,2},{2,3},{3,4},{4,5},{5,6},{6,7},{8,9},{9,10},{10,11},{11... | collective-permute-start | bytes 2408456 | tf_op jit(solution)/shard_map/ppermute | solution.py:322
  6.1 13.6 %collective-permute-start.1 = (bf16[2,784,256]{2,1,0:T(8,128)(2,1)}, bf16[2,784,256]{2,1,0:T(8,128)(2,1)S(1)}, u32[]{:S(2)}, u32[]{:S(2)}) collective-permute-start(bf16[2,784,256]{2,1,0:T(8,128)(2,1)} %pad_maximum_fusion.1), channel_id=1, source_target_pairs={{1,0},{2,1},{3,2},{4,3},{5,4},{6,5},{7,6},{9,8},{10,9},{11,10},{12... | collective-permute-start | bytes 2408456 | tf_op jit(solution)/shard_map/ppermute | solution.py:323
  32.3 34.0 %collective-permute-start.2 = (bf16[192,512]{1,0:T(8,128)(2,1)S(1)}, bf16[192,512]{1,0:T(8,128)(2,1)S(1)}, u32[]{:S(2)}, u32[]{:S(2)}) collective-permute-start(bf16[192,512]{1,0:T(8,128)(2,1)S(1)} %get-tuple-element.54), channel_id=1, source_target_pairs={{0,8},{8,0},{16,24},{24,16},{1,9},{9,1},{17,25},{25,17},{2,10},{10... | collective-permute-start | bytes 589832 | tf_op jit(solution)/shard_map/ppermute | solution.py:394
  33.8 33.0 %collective-permute-start.3 = (bf16[192,512]{1,0:T(8,128)(2,1)S(1)}, bf16[192,512]{1,0:T(8,128)(2,1)S(1)}, u32[]{:S(2)}, u32[]{:S(2)}) collective-permute-start(bf16[192,512]{1,0:T(8,128)(2,1)S(1)} %get-tuple-element.55), channel_id=1, source_target_pairs={{0,16},{8,24},{16,0},{24,8},{1,17},{9,25},{17,1},{25,9},{2,18},{10... | collective-permute-start | bytes 589832 | tf_op jit(solution)/shard_map/ppermute | solution.py:394
  35.3 33.0 %collective-permute-start.4 = (bf16[192,512]{1,0:T(8,128)(2,1)S(1)}, bf16[192,512]{1,0:T(8,128)(2,1)S(1)}, u32[]{:S(2)}, u32[]{:S(2)}) collective-permute-start(bf16[192,512]{1,0:T(8,128)(2,1)S(1)} %get-tuple-element.56), channel_id=1, source_target_pairs={{0,24},{8,16},{16,8},{24,0},{1,25},{9,17},{17,9},{25,1},{2,26},{10... | collective-permute-start | bytes 589832 | tf_op jit(solution)/shard_map/ppermute | solution.py:394
  44.9 24.8 %collective-permute-start.5 = (bf16[192,512]{1,0:T(8,128)(2,1)S(1)}, bf16[192,512]{1,0:T(8,128)(2,1)S(1)}, u32[]{:S(2)}, u32[]{:S(2)}) collective-permute-start(bf16[192,512]{1,0:T(8,128)(2,1)S(1)} %get-tuple-element.58), channel_id=1, source_target_pairs={{0,8},{8,0},{16,24},{24,16},{1,9},{9,1},{17,25},{25,17},{2,10},{10... | collective-permute-start | bytes 589832 | tf_op jit(solution)/shard_map/ppermute | solution.py:394
  46.4 23.8 %collective-permute-start.6 = (bf16[192,512]{1,0:T(8,128)(2,1)S(1)}, bf16[192,512]{1,0:T(8,128)(2,1)S(1)}, u32[]{:S(2)}, u32[]{:S(2)}) collective-permute-start(bf16[192,512]{1,0:T(8,128)(2,1)S(1)} %get-tuple-element.59), channel_id=1, source_target_pairs={{0,16},{8,24},{16,0},{24,8},{1,17},{9,25},{17,1},{25,9},{2,18},{10... | collective-permute-start | bytes 589832 | tf_op jit(solution)/shard_map/ppermute | solution.py:394
  66.8 11.4 %collective-permute-start.11 = (bf16[192,512]{1,0:T(8,128)(2,1)S(1)}, bf16[192,512]{1,0:T(8,128)(2,1)S(1)}, u32[]{:S(2)}, u32[]{:S(2)}) collective-permute-start(bf16[192,512]{1,0:T(8,128)(2,1)S(1)} %get-tuple-element.66), channel_id=1, source_target_pairs={{0,8},{8,0},{16,24},{24,16},{1,9},{9,1},{17,25},{25,17},{2,10},{10... | collective-permute-start | bytes 589832 | tf_op jit(solution)/shard_map/ppermute | solution.py:394
  69.8 13.6 %collective-permute-start.13 = (bf16[192,512]{1,0:T(8,128)(2,1)S(1)}, bf16[192,512]{1,0:T(8,128)(2,1)S(1)}, u32[]{:S(2)}, u32[]{:S(2)}) collective-permute-start(bf16[192,512]{1,0:T(8,128)(2,1)S(1)} %get-tuple-element.68), channel_id=1, source_target_pairs={{0,24},{8,16},{16,8},{24,0},{1,25},{9,17},{17,9},{25,1},{2,26},{10... | collective-permute-start | bytes 589832 | tf_op jit(solution)/shard_map/ppermute | solution.py:394
  70.3 16.4 %collective-permute-start.8 = (bf16[192,512]{1,0:T(8,128)(2,1)S(1)}, bf16[192,512]{1,0:T(8,128)(2,1)S(1)}, u32[]{:S(2)}, u32[]{:S(2)}) collective-permute-start(bf16[192,512]{1,0:T(8,128)(2,1)S(1)} %get-tuple-element.62), channel_id=1, source_target_pairs={{0,8},{8,0},{16,24},{24,16},{1,9},{9,1},{17,25},{25,17},{2,10},{10... | collective-permute-start | bytes 589832 | tf_op jit(solution)/shard_map/ppermute | solution.py:394
  74.9 12.5 %collective-permute-start.9 = (bf16[192,512]{1,0:T(8,128)(2,1)S(1)}, bf16[192,512]{1,0:T(8,128)(2,1)S(1)}, u32[]{:S(2)}, u32[]{:S(2)}) collective-permute-start(bf16[192,512]{1,0:T(8,128)(2,1)S(1)} %get-tuple-element.63), channel_id=1, source_target_pairs={{0,16},{8,24},{16,0},{24,8},{1,17},{9,25},{17,1},{25,9},{2,18},{10... | collective-permute-start | bytes 589832 | tf_op jit(solution)/shard_map/ppermute | solution.py:394
  78.2 13.0 %collective-permute-start.10 = (bf16[192,512]{1,0:T(8,128)(2,1)S(1)}, bf16[192,512]{1,0:T(8,128)(2,1)S(1)}, u32[]{:S(2)}, u32[]{:S(2)}) collective-permute-start(bf16[192,512]{1,0:T(8,128)(2,1)S(1)} %get-tuple-element.64), channel_id=1, source_target_pairs={{0,24},{8,16},{16,8},{24,0},{1,25},{9,17},{17,9},{25,1},{2,26},{10... | collective-permute-start | bytes 589832 | tf_op jit(solution)/shard_map/ppermute | solution.py:394
  101.0 24.4 %collective-permute-start.20 = (bf16[192,512]{1,0:T(8,128)(2,1)S(1)}, bf16[192,512]{1,0:T(8,128)(2,1)S(1)}, u32[]{:S(2)}, u32[]{:S(2)}) collective-permute-start(bf16[192,512]{1,0:T(8,128)(2,1)S(1)} %get-tuple-element.78), channel_id=1, source_target_pairs={{0,8},{8,0},{16,24},{24,16},{1,9},{9,1},{17,25},{25,17},{2,10},{10... | collective-permute-start | bytes 589832 | tf_op jit(solution)/shard_map/ppermute | solution.py:402
  101.6 53.0 %collective-permute-start.21 = (bf16[192,512]{1,0:T(8,128)(2,1)S(1)}, bf16[192,512]{1,0:T(8,128)(2,1)S(1)}, u32[]{:S(2)}, u32[]{:S(2)}) collective-permute-start(bf16[192,512]{1,0:T(8,128)(2,1)S(1)} %get-tuple-element.79), channel_id=1, source_target_pairs={{0,16},{8,24},{16,0},{24,8},{1,17},{9,25},{17,1},{25,9},{2,18},{10... | collective-permute-start | bytes 589832 | tf_op jit(solution)/shard_map/ppermute | solution.py:402
  111.8 16.0 %collective-permute-start.17 = (bf16[192,512]{1,0:T(8,128)(2,1)S(1)}, bf16[192,512]{1,0:T(8,128)(2,1)S(1)}, u32[]{:S(2)}, u32[]{:S(2)}) collective-permute-start(bf16[192,512]{1,0:T(8,128)(2,1)S(1)} %get-tuple-element.74), channel_id=1, source_target_pairs={{0,8},{8,0},{16,24},{24,16},{1,9},{9,1},{17,25},{25,17},{2,10},{10... | collective-permute-start | bytes 589832 | tf_op jit(solution)/shard_map/ppermute | solution.py:402
  113.4 15.0 %collective-permute-start.18 = (bf16[192,512]{1,0:T(8,128)(2,1)S(1)}, bf16[192,512]{1,0:T(8,128)(2,1)S(1)}, u32[]{:S(2)}, u32[]{:S(2)}) collective-permute-start(bf16[192,512]{1,0:T(8,128)(2,1)S(1)} %get-tuple-element.75), channel_id=1, source_target_pairs={{0,16},{8,24},{16,0},{24,8},{1,17},{9,25},{17,1},{25,9},{2,18},{10... | collective-permute-start | bytes 589832 | tf_op jit(solution)/shard_map/ppermute | solution.py:402
  114.9 14.0 %collective-permute-start.19 = (bf16[192,512]{1,0:T(8,128)(2,1)S(1)}, bf16[192,512]{1,0:T(8,128)(2,1)S(1)}, u32[]{:S(2)}, u32[]{:S(2)}) collective-permute-start(bf16[192,512]{1,0:T(8,128)(2,1)S(1)} %get-tuple-element.76), channel_id=1, source_target_pairs={{0,24},{8,16},{16,8},{24,0},{1,25},{9,17},{17,9},{25,1},{2,26},{10... | collective-permute-start | bytes 589832 | tf_op jit(solution)/shard_map/ppermute | solution.py:402
  125.3 29.3 %collective-permute-start.22 = (bf16[192,512]{1,0:T(8,128)(2,1)S(1)}, bf16[192,512]{1,0:T(8,128)(2,1)S(1)}, u32[]{:S(2)}, u32[]{:S(2)}) collective-permute-start(bf16[192,512]{1,0:T(8,128)(2,1)S(1)} %get-tuple-element.80), channel_id=1, source_target_pairs={{0,24},{8,16},{16,8},{24,0},{1,25},{9,17},{17,9},{25,1},{2,26},{10... | collective-permute-start | bytes 589832 | tf_op jit(solution)/shard_map/ppermute | solution.py:402
  127.8 13.2 %collective-permute-start.14 = (bf16[192,512]{1,0:T(8,128)(2,1)S(1)}, bf16[192,512]{1,0:T(8,128)(2,1)S(1)}, u32[]{:S(2)}, u32[]{:S(2)}) collective-permute-start(bf16[192,512]{1,0:T(8,128)(2,1)S(1)} %get-tuple-element.70), channel_id=1, source_target_pairs={{0,8},{8,0},{16,24},{24,16},{1,9},{9,1},{17,25},{25,17},{2,10},{10... | collective-permute-start | bytes 589832 | tf_op jit(solution)/shard_map/ppermute | solution.py:402
  128.4 13.3 %collective-permute-start.15 = (bf16[192,512]{1,0:T(8,128)(2,1)S(1)}, bf16[192,512]{1,0:T(8,128)(2,1)S(1)}, u32[]{:S(2)}, u32[]{:S(2)}) collective-permute-start(bf16[192,512]{1,0:T(8,128)(2,1)S(1)} %get-tuple-element.71), channel_id=1, source_target_pairs={{0,16},{8,24},{16,0},{24,8},{1,17},{9,25},{17,1},{25,9},{2,18},{10... | collective-permute-start | bytes 589832 | tf_op jit(solution)/shard_map/ppermute | solution.py:402
  128.9 13.3 %collective-permute-start.16 = (bf16[192,512]{1,0:T(8,128)(2,1)S(1)}, bf16[192,512]{1,0:T(8,128)(2,1)S(1)}, u32[]{:S(2)}, u32[]{:S(2)}) collective-permute-start(bf16[192,512]{1,0:T(8,128)(2,1)S(1)} %get-tuple-element.72), channel_id=1, source_target_pairs={{0,24},{8,16},{16,8},{24,0},{1,25},{9,17},{17,9},{25,1},{2,26},{10... | collective-permute-start | bytes 589832 | tf_op jit(solution)/shard_map/ppermute | solution.py:402
  141.1 18.5 %collective-permute-start.23 = (bf16[192,512]{1,0:T(8,128)(2,1)S(1)}, bf16[192,512]{1,0:T(8,128)(2,1)S(1)}, u32[]{:S(2)}, u32[]{:S(2)}) collective-permute-start(bf16[192,512]{1,0:T(8,128)(2,1)S(1)} %get-tuple-element.82), channel_id=1, source_target_pairs={{0,8},{8,0},{16,24},{24,16},{1,9},{9,1},{17,25},{25,17},{2,10},{10... | collective-permute-start | bytes 589832 | tf_op jit(solution)/shard_map/ppermute | solution.py:402
  141.7 17.9 %collective-permute-start.24 = (bf16[192,512]{1,0:T(8,128)(2,1)S(1)}, bf16[192,512]{1,0:T(8,128)(2,1)S(1)}, u32[]{:S(2)}, u32[]{:S(2)}) collective-permute-start(bf16[192,512]{1,0:T(8,128)(2,1)S(1)} %get-tuple-element.83), channel_id=1, source_target_pairs={{0,16},{8,24},{16,0},{24,8},{1,17},{9,25},{17,1},{25,9},{2,18},{10... | collective-permute-start | bytes 589832 | tf_op jit(solution)/shard_map/ppermute | solution.py:402
  142.2 17.4 %collective-permute-start.25 = (bf16[192,512]{1,0:T(8,128)(2,1)S(1)}, bf16[192,512]{1,0:T(8,128)(2,1)S(1)}, u32[]{:S(2)}, u32[]{:S(2)}) collective-permute-start(bf16[192,512]{1,0:T(8,128)(2,1)S(1)} %get-tuple-element.84), channel_id=1, source_target_pairs={{0,24},{8,16},{16,8},{24,0},{1,25},{9,17},{17,9},{25,1},{2,26},{10... | collective-permute-start | bytes 589832 | tf_op jit(solution)/shard_map/ppermute | solution.py:402
  (8 other events, 92.6 us)
